TPU v7x, 32 devices: a whole 2x2x4 slice. The times are simulated.
32 devices in a mesh: dp: 8 (over z, y), seq: 4 (over x, core).
Axes of the slice: x: 2, y: 2, z: 4, core: 2. Of those that a mesh axis runs over, the one named last changes fastest.
Arguments:
- tokens: bfloat16 [8, 512, 768], P('dp', 'seq'), may hold values from -6 to 6
- seg_ids: int32 [8, 512], P('dp', 'seq'), may hold values from 0 to 7, as said below
- slot_doc: int32 [8, 256], P('dp'), may hold values from 0 to 7, as said below
- proj_e: bfloat16 [512, 256], P('seq'), may hold values from -0.25 to 0.25
- g_attn: bfloat16 [768], replicated, may hold values from 0.5 to 1.5
- w_query: bfloat16 [768, 768], replicated, may hold values from -0.21875 to 0.21875
- w_key: bfloat16 [768, 768], replicated, may hold values from -0.21875 to 0.21875
- w_value: bfloat16 [768, 768], replicated, may hold values from -0.21875 to 0.21875
- w_out: bfloat16 [768, 768], replicated, may hold values from -0.875 to 0.875
- g_ffn: bfloat16 [768], replicated, may hold values from 0.5 to 1.5
- w_in: bfloat16 [768, 3072], replicated, may hold values from -0.21875 to 0.21875
- w_back: bfloat16 [3072, 768], replicated, may hold values from -0.109375 to 0.109375
- cotangent: bfloat16 [8, 512, 768], P('dp', 'seq'), may hold values from -6 to 6
Outputs:
- layer_out: bfloat16 [8, 512, 768], P('dp', 'seq')
- x_grad: float32 [8, 512, 768], P('dp', 'seq')
- g_attn_grad: float32 [768], P(('dp', 'seq'))
- w_query_grad: float32 [768, 768], P(('dp', 'seq'))
- w_key_grad: float32 [768, 768], P(('dp', 'seq'))
- w_value_grad: float32 [768, 768], P(('dp', 'seq'))
- w_out_grad: float32 [768, 768], P(('dp', 'seq'))
- g_ffn_grad: float32 [768], P(('dp', 'seq'))
- w_in_grad: float32 [768, 3072], P(('dp', 'seq'))
- w_back_grad: float32 [3072, 768], P(('dp', 'seq'))
- proj_e_grad: float32 [512, 256], P('seq', 'dp')
Inputs may be any that keep to these rules, and one draw needn't show every extreme that they name: `seg_ids`: along each row the ids never fall, and every id from 0 to 7 holds one position or more. `slot_doc`: in each row the ids 0 to 7 own consecutive blocks of slots in increasing order, each of one slot or more.
All inputs are finite; a program needn't handle non-finite values.
Results may differ from a plain program's by a relative error of at most 0.022.
Values may be sent and summed in bfloat16 or wider, within the bound.
A program may use at most 128 MiB of HBM per device.

v0:
```python
import jax
import jax.numpy as jnp
from jax import lax
from jax.sharding import PartitionSpec as P

HEAD_DIM = 64


def layer_norm(inputs, gain_vec):
    centre = inputs - jnp.mean(inputs, axis=-1, keepdims=True)
    spread = jnp.mean(centre * centre, axis=-1, keepdims=True)
    return centre * lax.rsqrt(spread + 1e-05) * gain_vec


def contract_rows(left_mat, right_mat):
    return lax.dot_general(
        left_mat, right_mat, (((0,), (0,)), ((), ())), preferred_element_type=jnp.float32
    )


def times_transposed(left_mat, right_mat):
    return lax.dot_general(
        left_mat, right_mat, (((1,), (1,)), ((), ())), preferred_element_type=jnp.float32
    )


def shards(
    tokens,
    seg_ids,
    slot_doc,
    proj_e,
    g_attn,
    w_query,
    w_key,
    w_value,
    w_out,
    g_ffn,
    w_in,
    w_back,
    cotangent,
):
    row_count, local_len, model_width = tokens.shape
    slot_count = proj_e.shape[1]
    head_count = model_width // HEAD_DIM
    token_count = row_count * local_len
    score_scale = HEAD_DIM ** (-0.5)
    x_flat = tokens.astype(jnp.float32).reshape(token_count, model_width)
    normed, norm_back = jax.vjp(layer_norm, x_flat, g_attn.astype(jnp.float32))
    normed_b = normed.astype(jnp.bfloat16)
    query_proj = jnp.dot(normed_b, w_query, preferred_element_type=jnp.float32).astype(jnp.bfloat16)
    key_proj = jnp.dot(normed_b, w_key, preferred_element_type=jnp.float32).astype(jnp.bfloat16)
    value_proj = jnp.dot(normed_b, w_value, preferred_element_type=jnp.float32).astype(jnp.bfloat16)
    select = seg_ids[:, :, None] == slot_doc[:, None, :]
    masked_e = jnp.where(select, proj_e[None, :, :], jnp.zeros((), jnp.bfloat16))
    key_rows = key_proj.reshape(row_count, local_len, model_width)
    value_rows = value_proj.reshape(row_count, local_len, model_width)
    key_piece = lax.all_gather(key_rows, "seq", axis=1, tiled=True)
    value_piece = lax.all_gather(value_rows, "seq", axis=1, tiled=True)
    e_piece = lax.all_gather(masked_e, "seq", axis=1, tiled=True)
    piece_count = key_piece.shape[1] // local_len
    key_split = key_piece.reshape(row_count, piece_count, local_len, model_width)
    value_split = value_piece.reshape(row_count, piece_count, local_len, model_width)
    e_split = e_piece.reshape(row_count, piece_count, local_len, slot_count)
    sum_keys = jnp.einsum(
        "rptj,rptd->rpjd", e_split, key_split, preferred_element_type=jnp.float32
    ).astype(jnp.bfloat16)
    sum_values = jnp.einsum(
        "rptj,rptd->rpjd", e_split, value_split, preferred_element_type=jnp.float32
    ).astype(jnp.bfloat16)
    summ_k = jnp.sum(sum_keys, axis=1, dtype=jnp.float32)
    summ_v = jnp.sum(sum_values, axis=1, dtype=jnp.float32)
    summ_kb = summ_k.astype(jnp.bfloat16).reshape(row_count, slot_count, head_count, HEAD_DIM)
    summ_vb = summ_v.astype(jnp.bfloat16).reshape(row_count, slot_count, head_count, HEAD_DIM)
    query_heads = query_proj.reshape(row_count, local_len, head_count, HEAD_DIM)
    raw_scores = jnp.einsum(
        "rthe,rjhe->rhtj", query_heads, summ_kb, preferred_element_type=jnp.float32
    )
    scores = jnp.where(select[:, None, :, :], raw_scores * score_scale, -1e30)
    row_max = jnp.max(scores, axis=-1, keepdims=True)
    exp_scores = jnp.exp(scores - row_max)
    attn_probs = exp_scores / jnp.sum(exp_scores, axis=-1, keepdims=True)
    probs_b = attn_probs.astype(jnp.bfloat16)
    context = jnp.einsum("rhtj,rjhe->rthe", probs_b, summ_vb, preferred_element_type=jnp.float32)
    context = context.reshape(token_count, model_width).astype(jnp.bfloat16)
    mid_rows = x_flat + jnp.dot(context, w_out, preferred_element_type=jnp.float32)
    normed_two, norm_two_back = jax.vjp(layer_norm, mid_rows, g_ffn.astype(jnp.float32))
    normed_two_b = normed_two.astype(jnp.bfloat16)
    hidden = jnp.dot(normed_two_b, w_in, preferred_element_type=jnp.float32)
    activated, gelu_back = jax.vjp(jax.nn.gelu, hidden)
    activated_b = activated.astype(jnp.bfloat16)
    result = mid_rows + jnp.dot(activated_b, w_back, preferred_element_type=jnp.float32)
    layer_out = result.astype(jnp.bfloat16).reshape(row_count, local_len, model_width)
    grad_top = cotangent.astype(jnp.float32).reshape(token_count, model_width)
    grad_top_b = grad_top.astype(jnp.bfloat16)
    grad_back_w = contract_rows(activated_b, grad_top_b)
    grad_act = times_transposed(grad_top_b, w_back)
    grad_hidden = gelu_back(grad_act)[0].astype(jnp.bfloat16)
    grad_in_w = contract_rows(normed_two_b, grad_hidden)
    grad_normed_two = times_transposed(grad_hidden, w_in)
    grad_mid, grad_g_ffn = norm_two_back(grad_normed_two)
    grad_mid = grad_mid + grad_top
    grad_mid_b = grad_mid.astype(jnp.bfloat16)
    grad_out_w = contract_rows(context, grad_mid_b)
    grad_context = times_transposed(grad_mid_b, w_out).astype(jnp.bfloat16)
    grad_context = grad_context.reshape(row_count, local_len, head_count, HEAD_DIM)
    grad_probs = jnp.einsum(
        "rthe,rjhe->rhtj", grad_context, summ_vb, preferred_element_type=jnp.float32
    )
    part_gv = jnp.einsum(
        "rhtj,rthe->rjhe", probs_b, grad_context, preferred_element_type=jnp.float32
    )
    grad_scores = attn_probs * (
        grad_probs - jnp.sum(attn_probs * grad_probs, axis=-1, keepdims=True)
    )
    grad_raw = (grad_scores * score_scale).astype(jnp.bfloat16)
    grad_query = jnp.einsum(
        "rhtj,rjhe->rthe", grad_raw, summ_kb, preferred_element_type=jnp.float32
    )
    grad_query = grad_query.reshape(token_count, model_width).astype(jnp.bfloat16)
    part_gk = jnp.einsum(
        "rhtj,rthe->rjhe", grad_raw, query_heads, preferred_element_type=jnp.float32
    )
    part_gk = part_gk.reshape(row_count, slot_count, model_width)
    part_gv = part_gv.reshape(row_count, slot_count, model_width)
    grad_sk, grad_sv = (
        lax.psum(part_gk.astype(jnp.bfloat16), "seq").astype(jnp.float32),
        lax.psum(part_gv.astype(jnp.bfloat16), "seq").astype(jnp.float32),
    )
    grad_sk_b = grad_sk.astype(jnp.bfloat16)
    grad_sv_b = grad_sv.astype(jnp.bfloat16)
    grad_keys = jnp.einsum("rtj,rjd->rtd", masked_e, grad_sk_b, preferred_element_type=jnp.float32)
    grad_keys = grad_keys.reshape(token_count, model_width).astype(jnp.bfloat16)
    grad_values = jnp.einsum(
        "rtj,rjd->rtd", masked_e, grad_sv_b, preferred_element_type=jnp.float32
    )
    grad_values = grad_values.reshape(token_count, model_width).astype(jnp.bfloat16)
    e_terms = jnp.einsum("rtd,rjd->rtj", key_rows, grad_sk_b, preferred_element_type=jnp.float32)
    e_terms = e_terms + jnp.einsum(
        "rtd,rjd->rtj", value_rows, grad_sv_b, preferred_element_type=jnp.float32
    )
    grad_e = jnp.sum(jnp.where(select, e_terms, 0.0), axis=0)
    grad_query_w = contract_rows(normed_b, grad_query)
    grad_key_w = contract_rows(normed_b, grad_keys)
    grad_value_w = contract_rows(normed_b, grad_values)
    grad_normed = times_transposed(grad_query, w_query) + times_transposed(grad_keys, w_key)
    grad_normed = grad_normed + times_transposed(grad_values, w_value)
    grad_input, grad_g_attn = norm_back(grad_normed)
    x_grad = (grad_input + grad_mid).reshape(row_count, local_len, model_width)
    shares = (
        lax.psum_scatter(grad_g_attn, ("dp", "seq"), scatter_dimension=0, tiled=True),
        lax.psum_scatter(grad_query_w, ("dp", "seq"), scatter_dimension=0, tiled=True),
        lax.psum_scatter(grad_key_w, ("dp", "seq"), scatter_dimension=0, tiled=True),
        lax.psum_scatter(grad_value_w, ("dp", "seq"), scatter_dimension=0, tiled=True),
        lax.psum_scatter(grad_out_w, ("dp", "seq"), scatter_dimension=0, tiled=True),
        lax.psum_scatter(grad_g_ffn, ("dp", "seq"), scatter_dimension=0, tiled=True),
        lax.psum_scatter(grad_in_w, ("dp", "seq"), scatter_dimension=0, tiled=True),
        lax.psum_scatter(grad_back_w, ("dp", "seq"), scatter_dimension=0, tiled=True),
    )
    e_share = lax.psum_scatter(grad_e, "dp", scatter_dimension=1, tiled=True)
    return (
        layer_out,
        x_grad,
        shares[0],
        shares[1],
        shares[2],
        shares[3],
        shares[4],
        shares[5],
        shares[6],
        shares[7],
        e_share,
    )


def solution(mesh):
    in_specs = (
        P("dp", "seq", None),
        P("dp", "seq"),
        P("dp", None),
        P("seq", None),
        P(),
        P(),
        P(),
        P(),
        P(),
        P(),
        P(),
        P(),
        P("dp", "seq", None),
    )
    out_specs = (
        P("dp", "seq", None),
        P("dp", "seq", None),
        P(("dp", "seq")),
        P(("dp", "seq"), None),
        P(("dp", "seq"), None),
        P(("dp", "seq"), None),
        P(("dp", "seq"), None),
        P(("dp", "seq")),
        P(("dp", "seq"), None),
        P(("dp", "seq"), None),
        P("seq", "dp"),
    )
    return jax.shard_map(shards, mesh=mesh, in_specs=in_specs, out_specs=out_specs, check_vma=False)
```

profile of v0, /device:TPU:0, one launch (start us, length us, event | category | flops | bytes accessed | tf_op | source)
XLA Modules:
  0.0 880.0 jit_solution(1225431284828325822)
XLA Ops:
  7.3 1.2 convert_reduce_fusion
  14.3 1.8 convolution_convert_fusion.7
  17.1 7.2 all-gather
  24.4 8.7 all-gather.1
  34.0 8.7 all-gather.2
  43.5 1.8 fusion.79
  45.3 2.0 convolution_convert_fusion.6
  49.6 1.9 fusion.9
  51.5 2.3 multiply_reduce_fusion.1
  55.7 2.6 convolution_convert_fusion.2
  58.3 1.6 fusion.81
  59.9 11.9 %fusion.22 = bf16[12,64,256]{2,1,0:T(8,128)(2,1)} fusion(bf16[128,12,64]{0,2,1:T(8,128)(2,1)S(1)} %bitcast.145, f32[12,128,256]{2,1,0:T(8,128)} %fusion.81, f32[12,128,256]{2,1,0:T(8,128)} %get-tuple-element.22, f32[12,128]{1,0:T(8,128)S(1)} %get-tuple-element.21), kind=kOutput, calls=%fused_computation.24 | convolution fusion | flops 53282560 | bytes 3741696 | tf_op jit(solution)/shard_map/rhtj,rthe->rjhe/dot_general | solution.py:120
  72.1 36.0 %all-reduce.6.cloned.1.call-done = (bf16[256,768]{0,1:T(8,128)(2,1)}, bf16[256,768]{0,1:T(8,128)(2,1)}) async-done(((bf16[256,768]{0,1:T(8,128)(2,1)}, bf16[256,768]{0,1:T(8,128)(2,1)}), (bf16[256,768]{0,1:T(8,128)(2,1)}, bf16[256,768]{0,1:T(8,128)(2,1)})) %all-reduce.6.cloned.1.call-update) | async-done | bytes 786448 | tf_op jit(solution)/shard_map/psum | solution.py:126
  108.1 1.3 fusion.84
  109.4 2.0 fusion.30
  111.5 1.9 fusion.83
  114.3 11.1 %fusion.26 = bf16[12,64,128]{2,1,0:T(8,128)(2,1)S(1)} fusion(bf16[256,12,64]{0,2,1:T(8,128)(2,1)S(1)} %bitcast.141, f32[12,128,256]{2,1,0:T(8,128)} %fusion.81, f32[12,128,256]{2,1,0:T(8,128)} %get-tuple-element.22, f32[12,128]{1,0:T(8,128)S(1)} %get-tuple-element.21), kind=kOutput, calls=%fused_computation.31 | convolution fusion | flops 53184256 | bytes 3741696 | tf_op jit(solution)/shard_map/rhtj,rjhe->rthe/dot_general | solution.py:116
  126.1 2.0 fusion.73
  130.2 2.1 fusion.69
  134.2 2.0 fusion.71
  136.3 1.3 copy-done.3
  137.6 5.2 fusion.51
  142.9 6.3 fusion.67
  149.2 1.9 fusion.82
  151.1 4.2 fusion.29
  157.6 39.6 %all-reduce.2 = (f32[768]{0:T(1024)S(1)}, f32[768]{0:T(1024)S(1)}) all-reduce(f32[768]{0:T(1024)S(1)} %get-tuple-element.13, f32[768]{0:T(1024)S(1)} %copy-done.29), channel_id=5, replica_groups=mesh['dp'=8,'seq'=4] {'dp','seq'}, use_global_device_ids=true, to_apply=%region_16.17.clone | all-reduce | flops 1536 | bytes 12288
  199.3 77.8 %reduce-scatter.14.cloned.1.call-done = f32[24,768]{1,0:T(8,128)} async-done(((f32[768,768]{1,0:T(8,128)}), f32[24,768]{1,0:T(8,128)}) %reduce-scatter.14.cloned.1.call-update) | async-done | bytes 73744 | tf_op jit(solution)/shard_map/reduce_scatter | solution.py:154
  277.1 104.5 %reduce-scatter.8.cloned.1.call-done = f32[24,768]{1,0:T(8,128)} async-done(((f32[768,768]{1,0:T(8,128)}), f32[24,768]{1,0:T(8,128)}) %reduce-scatter.8.cloned.1.call-update) | async-done | bytes 73744 | tf_op jit(solution)/shard_map/reduce_scatter | solution.py:151
  381.6 103.9 %reduce-scatter.12.cloned.1.call-done = f32[24,768]{1,0:T(8,128)} async-done(((f32[768,768]{1,0:T(8,128)}), f32[24,768]{1,0:T(8,128)}) %reduce-scatter.12.cloned.1.call-update) | async-done | bytes 73744 | tf_op jit(solution)/shard_map/reduce_scatter | solution.py:153
  485.5 104.5 %reduce-scatter.10.cloned.1.call-done = f32[24,768]{1,0:T(8,128)} async-done(((f32[768,768]{1,0:T(8,128)}), f32[24,768]{1,0:T(8,128)}) %reduce-scatter.10.cloned.1.call-update) | async-done | bytes 73744 | tf_op jit(solution)/shard_map/reduce_scatter | solution.py:152
  590.0 140.9 %reduce-scatter.18.cloned.1.call-done = f32[96,768]{1,0:T(8,128)} async-done(((f32[3072,768]{1,0:T(8,128)}), f32[96,768]{1,0:T(8,128)}) %reduce-scatter.18.cloned.1.call-update) | async-done | bytes 294928 | tf_op jit(solution)/shard_map/reduce_scatter | solution.py:157
  730.9 142.2 %reduce-scatter.16.cloned.1.call-done = f32[24,3072]{1,0:T(8,128)} async-done(((f32[768,3072]{1,0:T(8,128)}), f32[24,3072]{1,0:T(8,128)}) %reduce-scatter.16.cloned.1.call-update) | async-done | bytes 294928 | tf_op jit(solution)/shard_map/reduce_scatter | solution.py:156
  (138 shorter events, 22.8 us)
Async XLA Ops:
  7.2 40.2 %copy-start = (bf16[768,768]{1,0:T(8,128)(2,1)S(1)}, bf16[768,768]{1,0:T(8,128)(2,1)}, u32[]{:S(2)}) copy-start(bf16[768,768]{1,0:T(8,128)(2,1)} %param.21) | copy-start | bytes 3538948
  7.2 8.9 %copy-start.1 = (bf16[1,128,768]{2,1,0:T(8,128)(2,1)S(1)}, bf16[1,128,768]{2,1,0:T(8,128)(2,1)}, u32[]{:S(2)}) copy-start(bf16[1,128,768]{2,1,0:T(8,128)(2,1)} %param.13) | copy-start | bytes 589828
  7.2 8.9 %copy-start.6 = (bf16[768,768]{1,0:T(8,128)(2,1)S(1)}, bf16[768,768]{1,0:T(8,128)(2,1)}, u32[]{:S(2)}) copy-start(bf16[768,768]{1,0:T(8,128)(2,1)} %param.20) | copy-start | bytes 3538948
  7.2 100.9 %all-reduce.6.cloned.1.call-start = ((), (), s32[]{:S(2)}) async-start(), calls=%async_computation.14 | async-start | bytes 1572864 | tf_op jit(solution)/shard_map/psum | solution.py:126
  14.3 2.8 copy-start.18
  14.3 2.2 copy-start.4
  17.1 26.4 %copy-start.25 = (bf16[128,768]{0,1:T(8,128)(2,1)}, bf16[128,768]{0,1:T(8,128)(2,1)S(1)}, u32[]{:S(2)}) copy-start(bf16[128,768]{0,1:T(8,128)(2,1)S(1)} %copy.53) | copy-start | bytes 589828
  34.0 9.6 %copy-start.27 = (pred[128,256]{1,0:T(8,128)(4,1)S(1)}, pred[128,256]{1,0:T(8,128)(4,1)}, u32[]{:S(2)}) copy-start(pred[128,256]{1,0:T(8,128)(4,1)} %copy.52) | copy-start | bytes 98308
  43.5 3.9 copy-start.23
  43.5 4.6 slice-start
  45.3 2.8 slice-start.1
  45.3 4.0 slice-start.2
  47.4 1.6 copy-start.21
  47.4 2.2 slice-start.3
  47.9 5.9 copy-start.28
  48.1 5.7 copy-start.30
  49.6 1.9 copy-start.2
  51.5 2.3 copy-start.10
  59.9 49.5 %copy-start.31 = (s32[1,256]{1,0:T(1,128)S(1)}, s32[1,256]{1,0:T(1,128)}, u32[]{:S(2)}) copy-start(s32[1,256]{1,0:T(1,128)} %param.15) | copy-start | bytes 3076
  59.9 49.5 %copy-start.32 = (s32[1,128]{1,0:T(1,128)S(1)}, s32[1,128]{1,0:T(1,128)}, u32[]{:S(2)}) copy-start(s32[1,128]{1,0:T(1,128)} %param.14) | copy-start | bytes 1540
  71.8 39.7 %copy-start.22 = (bf16[12,64,128]{2,1,0:T(8,128)(2,1)S(1)}, bf16[12,64,128]{2,1,0:T(8,128)(2,1)}, u32[]{:S(2)}) copy-start(bf16[12,64,128]{2,1,0:T(8,128)(2,1)} %copy-done.21) | copy-start | bytes 589828
  71.8 127.4 %reduce-scatter.20.cloned.1.call-start = ((), (), s32[]{:S(2)}) async-start(), calls=%async_computation.13 | async-start | bytes 147456 | tf_op jit(solution)/shard_map/reduce_scatter | solution.py:159
  111.4 165.6 %reduce-scatter.14.cloned.1.call-start = ((), (), s32[]{:S(2)}) async-start(), calls=%async_computation.10 | async-start | bytes 2433024 | tf_op jit(solution)/shard_map/reduce_scatter | solution.py:154
  113.4 268.2 %reduce-scatter.8.cloned.1.call-start = ((), (), s32[]{:S(2)}) async-start(), calls=%async_computation.7 | async-start | bytes 2433024 | tf_op jit(solution)/shard_map/reduce_scatter | solution.py:151
  128.2 357.3 %reduce-scatter.12.cloned.1.call-start = ((), (), s32[]{:S(2)}) async-start(), calls=%async_computation.9 | async-start | bytes 2433024 | tf_op jit(solution)/shard_map/reduce_scatter | solution.py:153
  132.2 457.8 %reduce-scatter.10.cloned.1.call-start = ((), (), s32[]{:S(2)}) async-start(), calls=%async_computation.8 | async-start | bytes 2433024 | tf_op jit(solution)/shard_map/reduce_scatter | solution.py:152
  136.2 594.7 %reduce-scatter.18.cloned.1.call-start = ((), (), s32[]{:S(2)}) async-start(), calls=%async_computation.12 | async-start | bytes 9732096 | tf_op jit(solution)/shard_map/reduce_scatter | solution.py:157
  142.8 730.3 %reduce-scatter.16.cloned.1.call-start = ((), (), s32[]{:S(2)}) async-start(), calls=%async_computation.11 | async-start | bytes 9732096 | tf_op jit(solution)/shard_map/reduce_scatter | solution.py:156
  151.1 4.2 copy-start.5
  151.1 4.2 copy-start.15
  156.6 41.7 %copy-start.9 = (f32[128,768]{1,0:T(8,128)S(1)}, f32[128,768]{1,0:T(8,128)}, u32[]{:S(2)}) copy-start(f32[128,768]{1,0:T(8,128)} %copy-done.8) | copy-start | bytes 1179652
  156.6 41.7 %copy-start.34 = (f32[128]{0:T(128)S(1)}, f32[128]{0:T(128)}, u32[]{:S(2)}) copy-start(f32[128]{0:T(128)} %copy-done.33) | copy-start | bytes 1540
  (17 other events, 17.7 us)
Sparse Core Ops, SparseCore 0:
  72.0 36.0 all-reduce.5
  112.0 61.0 reduce-scatter.19
  178.9 98.1 reduce-scatter.13
  283.6 97.9 reduce-scatter.7
  387.3 98.1 reduce-scatter.11
  492.0 97.9 reduce-scatter.9
  596.5 134.3 reduce-scatter.17
  738.4 134.6 reduce-scatter.15
where the time goes:
time: 881 us; the launch traced here: 880 us
  waiting for transfers between devices  710 us (81%)
  matrix products  71.4 us (8%)
  blocking collectives  64.2 us (7%)
  between operations  14.7 us (2%)
  local copies, waits for them, and re-layouts  12 us (1%)
    reduce_scatter x1, waiting for transfers between devices, shards(): lax.psum_scatter(grad_in_w, ('dp', 'seq'), scatter_dimension=0, tiled=True)  142 us
    reduce_scatter x1, waiting for transfers between devices, shards(): lax.psum_scatter(grad_back_w, ('dp', 'seq'), scatter_dimension=0, tiled=T...  141 us
    reduce_scatter x1, waiting for transfers between devices, shards(): lax.psum_scatter(grad_key_w, ('dp', 'seq'), scatter_dimension=0, tiled=True)  105 us
    reduce_scatter x1, waiting for transfers between devices, shards(): lax.psum_scatter(grad_query_w, ('dp', 'seq'), scatter_dimension=0, tiled=...  105 us
    reduce_scatter x1, waiting for transfers between devices, shards(): lax.psum_scatter(grad_value_w, ('dp', 'seq'), scatter_dimension=0, tiled=...  104 us
    reduce_scatter x1, waiting for transfers between devices, shards(): lax.psum_scatter(grad_out_w, ('dp', 'seq'), scatter_dimension=0, tiled=True)  77.8 us
    unnamed x1, blocking collectives  39.6 us
    psum x1, waiting for transfers between devices, shards(): lax.psum(part_gk.astype(jnp.bfloat16), 'seq').astype(jnp.float32)  36 us
  transfers between devices with their start and end apart: 8, of which 7 were waited for; matrix products, arithmetic and copies ran while one was open for 5% of the time, Pallas kernels for 0%

commit v1 on v0

v1 whole, which is shorter than its diff:
```python
import functools
from types import SimpleNamespace

import jax
import jax.numpy as jnp
import numpy as np
from jax import lax
from jax.experimental import pallas as pl
from jax.experimental.pallas import tpu as pltpu
from jax.sharding import PartitionSpec as P

HEAD_DIM = 64
DP, SEQ = "dp", "seq"
BF = jnp.bfloat16
F32 = jnp.float32
MESH = pl.DeviceIdType.MESH
GELU_C = 0.7978845608028654
GELU_K = 0.044715


def nn(a, b):
    return lax.dot_general(a, b, (((1,), (0,)), ((), ())), preferred_element_type=F32)


def nt(a, b):
    return lax.dot_general(a, b, (((1,), (1,)), ((), ())), preferred_element_type=F32)


def selections(d_model, ff):
    unit = d_model // 16
    sel_a = np.zeros((2, d_model // 2, d_model), np.float32)
    sel_b = np.zeros((2, d_model // 2, d_model), np.float32)
    for x in range(2):
        for b in range(8):
            b2, b1, b0 = b // 4, (b // 2) % 2, b % 2
            for mat, j in ((sel_a, 4 * b0 + 2 * b1 + b2), (sel_b, 4 * b0 + 2 * b2 + b1)):
                for o in range(unit):
                    mat[x, b * unit + o, (2 * j + x) * unit + o] = 1
    q = ff // 32
    sel_c = np.zeros((2, 2, 2 * q, ff // 4), np.float32)
    for x in range(2):
        for c in range(2):
            for y in range(2):
                for o in range(q):
                    sel_c[x, c, y * q + o, (y * 4 + x * 2 + c) * q + o] = 1
    return sel_a, sel_b, sel_c


def layer_body(fused, r, sl):
    d, s = lax.axis_index(DP), lax.axis_index(SEQ)
    x, c = s // 2, s % 2
    y, lo, hi = d % 2, (d // 2) % 2, d // 4
    to_core = (d, s + 1 - 2 * c)
    to_x = (d, s + 2 - 4 * x)
    to_y = (d + 1 - 2 * y, s)
    to_lo = (d + 2 - 4 * lo, s)
    to_hi = (d + 4 - 8 * hi, s)
    lsem, ssem, rsem = r.lsem, r.ssem, r.rsem
    D = r.h1.shape[1]
    T = r.h1.shape[0]
    H = T // 2
    J = r.sk.shape[0]
    FC = D
    NF = r.w_in.shape[1] // FC
    HC = D // 2
    U = D // 16
    Q = r.wb.shape[2]
    scale = HEAD_DIM ** (-0.5)

    loads = []

    def load(src, dst):
        cp = pltpu.make_async_copy(src, dst, lsem.at[len(loads)])
        loads.append(cp)
        cp.start()
        return cp

    def rc(i, src, dst, dev):
        return pltpu.make_async_remote_copy(
            src_ref=src, dst_ref=dst, send_sem=ssem.at[i], recv_sem=rsem.at[i], device_id=dev, device_id_type=MESH
        )

    l_x = load(r.x_in, r.xb.at[pl.ds(0, H)])
    l_e = load(r.e_in, r.eb.at[pl.ds(0, H)])
    l_wq = load(r.wq_in, r.wq)
    l_wk = load(r.wk_in, r.wk)
    l_wv = load(r.wv_in, r.wv)
    l_dy = load(r.dy_in, r.dyb.at[pl.ds(0, H)])
    l_sa = load(r.sa_in.at[x], r.sa)
    l_sb = load(r.sb_in.at[x], r.sb)
    l_wo = load(r.wo_in, r.wo)
    l_sc0 = load(r.sc_in.at[x, c], r.sc.at[0])
    l_sc1 = load(r.sc_in.at[x, 1 - c], r.sc.at[1])
    l_w_in = load(r.w_in_in, r.w_in)
    l_w_back = load(r.w_back_in, r.w_back)

    partners = [to_core, to_x] + ([to_y, to_lo, to_hi] if fused else [])
    barrier = pltpu.get_barrier_semaphore()
    for dev in partners:
        pl.semaphore_signal(barrier, inc=1, device_id=dev, device_id_type=MESH)
    r.segf[0] = jnp.broadcast_to(r.seg_in[...].astype(F32), (8, H))
    pl.semaphore_wait(barrier, len(partners))

    x_seg = rc(sl.x_seg, r.segf.at[0], r.segf.at[1], to_x)
    x_e = rc(sl.x_e, r.e_in, r.eb.at[pl.ds(H, H)], to_x)
    x_x = rc(sl.x_x, r.x_in, r.xb.at[pl.ds(H, H)], to_x)
    x_dy = rc(sl.x_dy, r.dy_in, r.dyb.at[pl.ds(H, H)], to_x)
    x_x.start()
    x_seg.start()
    x_e.start()

    rows_i = lax.broadcasted_iota(jnp.int32, (T, T), 0)
    cols_i = lax.broadcasted_iota(jnp.int32, (T, T), 1)
    r.eye[...] = jnp.where(rows_i == cols_i, 1.0, 0.0).astype(BF)
    ga = r.ga[...].astype(F32)
    gf = r.gf[...].astype(F32)
    inv_d = 1.0 / D

    def norm_rows(v):
        cen = v - jnp.sum(v, axis=1, keepdims=True) * inv_d
        rstd = lax.rsqrt(jnp.sum(cen * cen, axis=1, keepdims=True) * inv_d + 1e-5)
        return cen * rstd, rstd

    NR = 64

    def norm_one(i):
        rows = pl.ds(pl.multiple_of(i * NR, NR), NR)
        xh, rstd = norm_rows(r.xb[rows, :].astype(F32))
        r.xh1[rows, :] = xh
        r.rs1[rows, :] = jnp.broadcast_to(rstd, (NR, 128))
        r.h1[rows, :] = (xh * ga).astype(BF)

    l_x.wait()

    @pl.loop(0, 2)
    def _(p):
        @pl.when(p == 1)
        def _():
            x_x.wait()
            x_dy.start()

        @pl.loop(0, H // NR)
        def _(i):
            norm_one(p * (H // NR) + i)

        @pl.when(p == 0)
        def _():
            l_wq.wait()
            l_wk.wait()
            l_wv.wait()

        rows = pl.ds(pl.multiple_of(p * H, H), H)
        h = r.h1[rows, :]
        r.q[rows, :] = nn(h, r.wq[...]).astype(BF)
        r.k[rows, :] = nn(h, r.wk[...]).astype(BF)
        r.v[rows, :] = nn(h, r.wv[...]).astype(BF)

    x_seg.wait()
    x_e.wait()
    l_e.wait()
    seg_row = jnp.concatenate([r.segf[0, 0:1, :], r.segf[1, 0:1, :]], axis=1)
    slot_row = r.slot_in[...].astype(F32)
    eye = r.eye[...]
    zero = jnp.zeros((), BF)
    seg_col = nt(eye, jnp.broadcast_to(seg_row, (J, T)).astype(BF))
    slot_col = nt(eye, jnp.broadcast_to(slot_row, (T, J)).astype(BF))
    r.sel_t[...] = jnp.where(slot_col == seg_row, 1.0, 0.0)
    r.me[...] = jnp.where(seg_col == slot_row, r.eb[...].astype(F32), 0.0).astype(BF)
    r.met[...] = nt(eye, r.me[...]).astype(BF)

    r.pk[0] = nn(r.met[...], r.k[...]).astype(BF)
    c_pk = rc(sl.c_pk, r.pk.at[0], r.pkr.at[0], to_core)
    c_pk.start()
    r.pk[1] = nn(r.met[...], r.v[...]).astype(BF)
    c_pv = rc(sl.c_pv, r.pk.at[1], r.pkr.at[1], to_core)
    c_pv.start()
    l_sa.wait()
    l_sb.wait()
    r.h1t[0] = nt(r.sb[...], r.h1[...]).astype(BF)
    c_h1t = rc(sl.c_h1t, r.h1t.at[0], r.h1t.at[1], to_core)
    c_h1t.start()
    c_pk.wait()
    r.sk[...] = (r.pk[0].astype(F32) + r.pkr[0].astype(F32)).astype(BF)
    c_pv.wait()
    r.sv[...] = (r.pk[1].astype(F32) + r.pkr[1].astype(F32)).astype(BF)

    lane = lax.broadcasted_iota(jnp.int32, (T, 128), 1)
    head_mask = [jnp.where(lane < 64, 1.0, 0.0).astype(BF), jnp.where(lane < 64, 0.0, 1.0).astype(BF)]

    @pl.loop(0, D // 128)
    def _(i):
        cols = pl.ds(pl.multiple_of(i * 128, 128), 128)
        q2, sk2, sv2 = r.q[:, cols], r.sk[:, cols], r.sv[:, cols]
        r.skt[cols, :] = nt(r.eye[0:128, 0:128], sk2).astype(BF)
        r.svt[...] = nt(r.eye[0:128, 0:128], sv2).astype(BF)
        for h in range(2):
            raw = nt(sk2, q2 * head_mask[h])
            sc = jnp.where(r.sel_t[...] > 0.5, raw * scale, -1e30)
            e = jnp.exp(sc - jnp.max(sc, axis=0, keepdims=True))
            pt = (e * (1.0 / jnp.sum(e, axis=0, keepdims=True))).astype(BF)
            r.pt[i, :, h * T : (h + 1) * T] = pt
            r.ctxt[pl.ds(pl.multiple_of(i * 128 + h * 64, 64), 64), :] = nn(
                r.svt[h * 64 : (h + 1) * 64, :], pt
            ).astype(BF)
        r.ctx[:, cols] = nt(r.eye[...], r.ctxt[cols, :]).astype(BF)

    l_wo.wait()

    @pl.loop(0, 2)
    def _(p):
        rows = pl.ds(pl.multiple_of(p * H, H), H)
        r.mid[rows, :] = r.xb[rows, :].astype(F32) + nn(r.ctx[rows, :], r.wo[...])

    @pl.loop(0, T // NR)
    def _(i):
        rows = pl.ds(pl.multiple_of(i * NR, NR), NR)
        xh, rstd = norm_rows(r.mid[rows, :])
        r.xh2[rows, :] = xh
        r.rs2[rows, :] = jnp.broadcast_to(rstd, (NR, 128))
        r.h2[rows, :] = (xh * gf).astype(BF)

    r.h2t[0] = nt(r.sa[...], r.h2[...]).astype(BF)
    c_h2t = rc(sl.c_h2t, r.h2t.at[0], r.h2t.at[1], to_core)
    c_h2t.start()
    x_dy.wait()
    l_dy.wait()
    c_dy = rc(sl.c_dy, r.dyb, r.dyo, to_core)
    c_dy.start()
    r.ctt[0] = nn(r.sb[...], r.ctxt[...]).astype(BF)
    c_ctt = rc(sl.c_ctt, r.ctt.at[0], r.ctt.at[1], to_core)
    c_ctt.start()
    l_w_in.wait()
    l_w_back.wait()
    l_sc0.wait()
    l_sc1.wait()

    def c_at(f):
        return rc(sl.c_at + f, r.at.at[f, 1], r.atr.at[f], to_core)

    def c_du(f):
        return rc(sl.c_du + f, r.du.at[f, 1 - c], r.dur.at[f], to_core)

    def y_wb(f):
        return rc(sl.y_wb + f, r.wb.at[f, 1 - y], r.wb1.at[f], to_y)

    def y_wi(f):
        return rc(sl.y_wi + f, r.wi.at[f, pl.ds(pl.multiple_of((1 - y) * 4 * U, 16), 4 * U)], r.wi1.at[f], to_y)

    SB = 256

    @pl.loop(0, NF + 1)
    def _(f):
        @pl.when(f < NF)
        def _():
            for b in range(FC // SB):
                off = pl.multiple_of(f * FC + b * SB, SB)
                u = nn(r.h2[...], r.w_in[:, pl.ds(off, SB)])
                g = nt(r.dyb[...], r.w_back[pl.ds(off, SB), :])
                u2 = u * u
                th = jnp.tanh(GELU_C * (u + GELU_K * (u2 * u)))
                half = 0.5 * (1.0 + th)
                r.a[:, b * SB : (b + 1) * SB] = (u * half).astype(BF)
                slope = half + 0.5 * u * (1.0 - th * th) * (GELU_C * (1.0 + 3.0 * GELU_K * u2))
                r.duf[:, b * SB : (b + 1) * SB] = (slope * g).astype(BF)
            r.du[f, 0] = r.duf[:, 0:HC]
            r.du[f, 1] = r.duf[:, HC : 2 * HC]
            c_du(f).start()
            r.at[f, 0] = nt(r.sc[0], r.a[...]).astype(BF)
            r.at[f, 1] = nt(r.sc[1], r.a[...]).astype(BF)
            c_at(f).start()
            rows = pl.ds(pl.multiple_of(f * FC, FC), FC)
            part_o = nn(r.a[0:H, :], r.w_back[rows, :])
            part_d = nt(r.duf[...], r.w_in[:, rows])

            @pl.when(f == 0)
            def _():
                c_dy.wait()
                c_h2t.wait()
                r.oacc[...] = part_o
                r.dacc[...] = part_d

            @pl.when(f > 0)
            def _():
                r.oacc[...] += part_o
                r.dacc[...] += part_d

        @pl.when(f > 0)
        def _():
            g = f - 1
            c_at(g).wait()
            wb = nn(r.at[g, 0], r.dyb[...]) + nn(r.atr[g], r.dyo[...])
            r.wb[g, 0] = wb[0:Q, :].astype(BF)
            r.wb[g, 1] = wb[Q : 2 * Q, :].astype(BF)
            if fused:
                y_wb(g).start()
            c_du(g).wait()
            wi = nn(r.h2t[0], r.du[g, c]) + nn(r.h2t[1], r.dur[g])
            r.wi[g] = wi.astype(BF)
            if fused:
                y_wi(g).start()

    def add_into(dst, idx, src):
        dst[idx] = (dst[idx].astype(F32) + src.astype(F32)).astype(BF)

    def lo_wb(p):
        return rc(sl.lo_wb + p, r.wb.at[2 * p + 1 - lo, y], r.wb2.at[p], to_lo)

    def hi_wb():
        return rc(sl.hi_wb, r.wb.at[2 * (1 - hi) + lo, y], r.wb3, to_hi)

    def wi_rows(start, count):
        return pl.ds(pl.multiple_of(start, 16), count)

    def lo_wi(f):
        return rc(sl.lo_wi + f, r.wi.at[f, wi_rows(y * 4 * U + (1 - lo) * 2 * U, 2 * U)], r.wi2.at[f], to_lo)

    def hi_wi(f):
        return rc(
            sl.hi_wi + f, r.wi.at[f, wi_rows(y * 4 * U + lo * 2 * U + (1 - hi) * U, U)], r.wi3.at[f], to_hi
        )

    def pump_wb1(p):
        for e in range(2):
            f = 2 * p + e
            y_wb(f).wait()
            add_into(r.wb, (f, y), r.wb1[f])
        lo_wb(p).start()

    def pump_wi1(f):
        y_wi(f).wait()
        add_into(r.wi, (f, wi_rows(y * 4 * U, 4 * U), slice(None)), r.wi1[f])
        lo_wi(f).start()

    def pump_wb2():
        for p in range(2):
            lo_wb(p).wait()
            add_into(r.wb, (2 * p + lo, y), r.wb2[p])
        hi_wb().start()

    def pump_wi2(f):
        lo_wi(f).wait()
        add_into(r.wi, (f, wi_rows(y * 4 * U + lo * 2 * U, 2 * U), slice(None)), r.wi2[f])
        hi_wi(f).start()

    GN = r.gq.shape[1]
    EB = J // 8

    def st_rows(unit, stage):
        base = [0, lo * 4 * unit, lo * 4 * unit + y * 2 * unit][stage]
        n = [4, 2, 1][stage] * unit
        bit = [lo, y, hi][stage]
        return base + bit * n, base + (1 - bit) * n, n

    if fused:
        chain_o = (r.go, (r.go1, r.go2, r.go3), sl.go, U)
        chain_q = (r.gq, (r.gq1, r.gq2, r.gq3), sl.gq, U)
        chain_e = (r.ge, (r.ge1, r.ge2, r.ge3), sl.ge, EB)

    def st_copy(chain, stage):
        buf, got, slot, unit = chain
        _, sent, n = st_rows(unit, stage)
        dev = [to_lo, to_y, to_hi][stage]
        return rc(slot + stage, buf.at[pl.ds(pl.multiple_of(sent, 16), n)], got[stage], dev)

    def st_add(chain, stage):
        buf, got, _, unit = chain
        st_copy(chain, stage).wait()
        kept, _, n = st_rows(unit, stage)
        add_into(buf, (pl.ds(pl.multiple_of(kept, 16), n), slice(None)), got[stage][...])

    def st_last(chain):
        buf, got, _, unit = chain
        st_copy(chain, 2).wait()
        kept, _, n = st_rows(unit, 2)
        return buf[pl.ds(pl.multiple_of(kept, 16), n), :].astype(F32) + got[2][...].astype(F32)

    @pl.loop(0, T // NR)
    def _(i):
        rows = pl.ds(pl.multiple_of(i * NR, NR), NR)
        dn, xh = r.dacc[rows, :], r.xh2[rows, :]
        part = jnp.sum(dn * xh, axis=0, keepdims=True)

        @pl.when(i == 0)
        def _():
            r.gv[1:2, :] = part

        @pl.when(i > 0)
        def _():
            r.gv[1:2, :] += part

        dg = dn * gf
        m1 = jnp.sum(dg, axis=1, keepdims=True) * inv_d
        m2 = jnp.sum(dg * xh, axis=1, keepdims=True) * inv_d
        dmid = r.dyb[rows, :].astype(F32) + r.rs2[rows, 0:1] * (dg - m1 - xh * m2)
        r.dmid[rows, :] = dmid
        b = dmid.astype(BF)
        r.dmb[0, rows, :] = b[:, 0:HC]
        r.dmb[1, rows, :] = b[:, HC : 2 * HC]

    r.o_layer[...] = (r.mid[0:H, :] + r.oacc[...]).astype(BF)
    c_dm = rc(sl.c_dm, r.dmb.at[1 - c], r.dmr, to_core)
    c_dm.start()
    r.dctx[...] = (nt(r.dmb[0], r.wo[:, 0:HC]) + nt(r.dmb[1], r.wo[:, HC : 2 * HC])).astype(BF)
    c_ctt.wait()
    c_dm.wait()
    r.go[...] = (nn(r.ctt[0], r.dmb[c]) + nn(r.ctt[1], r.dmr[...])).astype(BF)
    if fused:
        st_copy(chain_o, 0).start()

    def c_ds(i):
        return rc(sl.c_ds + i, r.pd.at[i], r.pdr.at[i], to_core)

    @pl.loop(0, D // 128)
    def _(i):
        cols = pl.ds(pl.multiple_of(i * 128, 128), 128)
        q2, dc2, sv2 = r.q[:, cols], r.dctx[:, cols], r.sv[:, cols]
        dsv = None
        dsk = None
        for h in range(2):
            dch = dc2 * head_mask[h]
            ptb = r.pt[i, :, h * T : (h + 1) * T]
            dp = nt(sv2, dch)
            pf = ptb.astype(F32)
            ds = pf * (dp - jnp.sum(pf * dp, axis=0, keepdims=True))
            draw = (ds * scale).astype(BF)
            av = nn(ptb, dch)
            ak = nn(draw, q2 * head_mask[h])
            dsv = av if dsv is None else dsv + av
            dsk = ak if dsk is None else dsk + ak
            r.dqt[h * 64 : (h + 1) * 64, :] = nn(
                r.skt[pl.ds(pl.multiple_of(i * 128 + h * 64, 64), 64), :], draw
            ).astype(BF)
        r.pd[i, 0] = dsk.astype(BF)
        r.pd[i, 1] = dsv.astype(BF)
        c_ds(i).start()
        r.dq[:, cols] = nt(r.eye[...], r.dqt[...]).astype(BF)
        if fused:
            for f in range(2):
                @pl.when(i == 1 + 2 * f)
                def _():
                    pump_wi1(f)
            @pl.when(i == 4)
            def _():
                pump_wb1(0)

    @pl.loop(0, D // 128)
    def _(i):
        cols = pl.ds(pl.multiple_of(i * 128, 128), 128)
        c_ds(i).wait()
        r.dsk[:, cols] = (r.pd[i, 0].astype(F32) + r.pdr[i, 0].astype(F32)).astype(BF)
        r.dsv[:, cols] = (r.pd[i, 1].astype(F32) + r.pdr[i, 1].astype(F32)).astype(BF)

    def c_g(i):
        return rc(sl.c_g + i, r.dqkv.at[i, 1 - c], r.dqr.at[i], to_core)

    r.dqkv[0, 0] = r.dq[:, 0:HC]
    r.dqkv[0, 1] = r.dq[:, HC : 2 * HC]
    c_g(0).start()
    dk = nn(r.me[...], r.dsk[...]).astype(BF)
    r.dqkv[1, 0] = dk[:, 0:HC]
    r.dqkv[1, 1] = dk[:, HC : 2 * HC]
    c_g(1).start()
    dv = nn(r.me[...], r.dsv[...]).astype(BF)
    r.dqkv[2, 0] = dv[:, 0:HC]
    r.dqkv[2, 1] = dv[:, HC : 2 * HC]
    c_g(2).start()

    de = nt(r.dsk[...], r.k[0:H, :]) + nt(r.dsv[...], r.v[0:H, :])
    de = jnp.where(r.sel_t[:, 0:H] > 0.5, de, 0.0).astype(BF)
    for b in range(8):
        b2, b1, b0 = b // 4, (b // 2) % 2, b % 2
        j = 4 * b0 + 2 * b2 + b1
        r.ge[b * EB : (b + 1) * EB, :] = de[j * EB : (j + 1) * EB, :]

    for i, w in enumerate((r.wq, r.wk, r.wv)):
        for hf in range(2):
            part = nt(r.dqkv[i, hf], w[:, hf * HC : (hf + 1) * HC])
            if i == 0 and hf == 0:
                r.dacc[...] = part
            else:
                r.dacc[...] += part

    @pl.loop(0, T // NR)
    def _(i):
        rows = pl.ds(pl.multiple_of(i * NR, NR), NR)
        dn, xh = r.dacc[rows, :], r.xh1[rows, :]
        part = jnp.sum(dn * xh, axis=0, keepdims=True)

        @pl.when(i == 0)
        def _():
            r.gv[0:1, :] = part

        @pl.when(i > 0)
        def _():
            r.gv[0:1, :] += part

        @pl.when(i < H // NR)
        def _():
            dg = dn * ga
            m1 = jnp.sum(dg, axis=1, keepdims=True) * inv_d
            m2 = jnp.sum(dg * xh, axis=1, keepdims=True) * inv_d
            r.o_x[rows, :] = r.dmid[rows, :] + r.rs1[rows, 0:1] * (dg - m1 - xh * m2)

    gv = jnp.concatenate([r.gv[0:2, :], jnp.zeros((126, D), F32)], axis=0).astype(BF)
    r.gq[:, 3 * HC : GN] = nt(r.sb[...], gv).astype(BF)

    c_h1t.wait()
    for i in range(3):
        c_g(i).wait()
        r.gq[:, i * HC : (i + 1) * HC] = (
            nn(r.h1t[0], r.dqkv[i, c]) + nn(r.h1t[1], r.dqr[i])
        ).astype(BF)

    if not fused:
        return

    st_copy(chain_q, 0).start()
    st_copy(chain_e, 0).start()

    st_add(chain_o, 0)
    st_copy(chain_o, 1).start()
    pump_wi1(2)
    pump_wb1(1)
    pump_wi1(3)
    st_add(chain_q, 0)
    st_copy(chain_q, 1).start()
    st_add(chain_e, 0)
    st_copy(chain_e, 1).start()
    for f in range(NF):
        pump_wi2(f)
    pump_wb2()
    st_add(chain_o, 1)
    st_copy(chain_o, 2).start()
    st_add(chain_q, 1)
    st_copy(chain_q, 2).start()
    st_add(chain_e, 1)
    st_copy(chain_e, 2).start()

    fin = r.fin
    for f in range(NF):
        hi_wi(f).wait()
        own = r.wi[f, wi_rows(y * 4 * U + lo * 2 * U + hi * U, U), :]
        fin[:, f * HC : (f + 1) * HC] = own.astype(F32) + r.wi3[f].astype(F32)
    at = NF * HC
    fin[:, at : at + HC] = st_last(chain_o)
    fin[:, at + HC : at + HC + GN] = st_last(chain_q)
    at += HC + GN
    half = U // 2
    c_fin = rc(sl.c_fin, fin.at[pl.ds(pl.multiple_of((1 - c) * half, 8), half)], r.finr, to_core)
    c_fin.start()
    hi_wb().wait()
    r.o_back[...] = r.wb[2 * hi + lo, y].astype(F32) + r.wb3[...].astype(F32)
    r.o_e[...] = st_last(chain_e)
    c_fin.wait()
    mine = pl.ds(pl.multiple_of(c * half, 8), half)

    def put(dst, base, src_col):
        dst[:, pl.ds(pl.multiple_of(base + c * HC, 128), HC)] = fin[mine, src_col : src_col + HC]
        dst[:, pl.ds(pl.multiple_of(base + (1 - c) * HC, 128), HC)] = r.finr[:, src_col : src_col + HC]

    for f in range(NF):
        put(r.o_in, f * FC, f * HC)
    for i, dst in enumerate((r.o_out, r.o_q, r.o_k, r.o_v)):
        put(dst, 0, (NF + i) * HC)
    r.o_g[...] = fin[mine, at - 128 : at] + r.finr[:, at - 128 : at]


def run_layer(mesh_shape, tokens, seg_ids, slot_doc, proj_e, g_attn, w_query, w_key, w_value, w_out, g_ffn, w_in,
              w_back, cotangent):
    n_dp, n_seq = mesh_shape
    rows, H, D = tokens.shape
    J = proj_e.shape[1]
    FF = w_in.shape[1]
    fused = n_dp == 8
    T = 2 * H
    HC, U, NF, Q = D // 2, D // 16, FF // D, FF // 32
    EB = J // 8
    GN = 3 * HC + 128
    sel_a, sel_b, sel_c = (jnp.asarray(m, BF) for m in selections(D, FF))

    inputs = dict(
        x_in=(tokens.reshape(H, D), False),
        seg_in=(seg_ids.reshape(1, H), True),
        slot_in=(slot_doc.reshape(1, J), True),
        e_in=(proj_e, False),
        ga=(g_attn.reshape(1, D), True),
        wq_in=(w_query, False),
        wk_in=(w_key, False),
        wv_in=(w_value, False),
        wo_in=(w_out, False),
        gf=(g_ffn.reshape(1, D), True),
        w_in_in=(w_in, False),
        w_back_in=(w_back, False),
        dy_in=(cotangent.reshape(H, D), False),
        sa_in=(sel_a, False),
        sb_in=(sel_b, False),
        sc_in=(sel_c, False),
    )
    parts = dict(
        wb=((NF, 2, Q, D), BF),
        wi=((NF, D // 2, HC), BF),
        go=((D // 2, HC), BF),
        gq=((D // 2, GN), BF),
        ge=((J, H), BF),
    )
    outs = dict(o_layer=((H, D), BF), o_x=((H, D), F32))
    if fused:
        outs.update(
            o_g=((U // 2, 128), F32),
            o_q=((U // 2, D), F32),
            o_k=((U // 2, D), F32),
            o_v=((U // 2, D), F32),
            o_out=((U // 2, D), F32),
            o_in=((U // 2, FF), F32),
            o_back=((Q, D), F32),
            o_e=((EB, H), F32),
        )
    else:
        outs.update(parts)
    scratch = dict(
        xb=((T, D), BF), eb=((T, J), BF), segf=((2, 8, H), F32),
        wq=((D, D), BF), wk=((D, D), BF), wv=((D, D), BF), wo=((D, D), BF),
        w_in=((D, FF), BF), w_back=((FF, D), BF),
        dyb=((T, D), BF), dyo=((T, D), BF),
        sa=((D // 2, D), BF), sb=((D // 2, D), BF), sc=((2, 2 * Q, FF // 4), BF),
        eye=((T, T), BF),
        h1=((T, D), BF), xh1=((T, D), F32), rs1=((T, 128), F32),
        q=((T, D), BF), k=((T, D), BF), v=((T, D), BF),
        sel_t=((J, T), F32), me=((T, J), BF), met=((J, T), BF),
        pk=((2, J, D), BF), pkr=((2, J, D), BF), sk=((J, D), BF), sv=((J, D), BF),
        skt=((D, J), BF), svt=((128, J), BF),
        pt=((D // 128, J, 2 * T), BF), ctxt=((D, T), BF), ctx=((T, D), BF),
        mid=((T, D), F32), xh2=((T, D), F32), rs2=((T, 128), F32), h2=((T, D), BF),
        h1t=((2, D // 2, T), BF), h2t=((2, D // 2, T), BF), ctt=((2, D // 2, T), BF),
        a=((T, D), BF), duf=((T, D), BF), du=((NF, 2, T, HC), BF), dur=((NF, T, HC), BF),
        at=((NF, 2, 2 * Q, T), BF), atr=((NF, 2 * Q, T), BF),
        oacc=((H, D), F32), dacc=((T, D), F32), dmid=((T, D), F32), gv=((8, D), F32),
        dmb=((2, T, HC), BF), dmr=((T, HC), BF), dctx=((T, D), BF),
        dqt=((128, T), BF), dq=((T, D), BF),
        pd=((D // 128, 2, J, 128), BF), pdr=((D // 128, 2, J, 128), BF),
        dsk=((J, D), BF), dsv=((J, D), BF),
        dqkv=((3, 2, T, HC), BF), dqr=((3, T, HC), BF),
    )
    if fused:
        scratch.update(
            parts,
            wb1=((NF, Q, D), BF), wb2=((2, Q, D), BF), wb3=((Q, D), BF),
            wi1=((NF, 4 * U, HC), BF), wi2=((NF, 2 * U, HC), BF), wi3=((NF, U, HC), BF),
            go1=((4 * U, HC), BF), go2=((2 * U, HC), BF), go3=((U, HC), BF),
            gq1=((4 * U, GN), BF), gq2=((2 * U, GN), BF), gq3=((U, GN), BF),
            ge1=((4 * EB, H), BF), ge2=((2 * EB, H), BF), ge3=((EB, H), BF),
            fin=((U, NF * HC + HC + GN), F32), finr=((U // 2, NF * HC + HC + GN), F32),
        )
    counts = dict(
        x_seg=1, x_e=1, x_x=1, x_dy=1, c_pk=1, c_pv=1, c_h1t=1, c_h2t=1, c_dy=1, c_ctt=1, c_at=NF, c_du=NF, c_dm=1,
        c_ds=D // 128, c_g=3, y_wb=NF, y_wi=NF, lo_wb=2, lo_wi=NF, hi_wb=1, hi_wi=NF, go=3, gq=3, ge=3, c_fin=1,
    )
    sl, count = SimpleNamespace(), 0
    for name, n in counts.items():
        setattr(sl, name, count)
        count += n
    names = [*inputs, *outs, *scratch]

    def body(*refs):
        r = SimpleNamespace(**dict(zip(names, refs)))
        r.lsem, r.ssem, r.rsem = refs[len(names) :]
        layer_body(fused, r, sl)

    res = pl.pallas_call(
        body,
        out_shape=[jax.ShapeDtypeStruct(sh, dt) for sh, dt in outs.values()],
        in_specs=[pl.BlockSpec(memory_space=pltpu.VMEM if v else pl.ANY) for _, v in inputs.values()],
        out_specs=[pl.BlockSpec(memory_space=pltpu.VMEM) for _ in outs],
        scratch_shapes=[pltpu.VMEM(sh, dt) for sh, dt in scratch.values()]
        + [pltpu.SemaphoreType.DMA((13,)), pltpu.SemaphoreType.DMA((count,)), pltpu.SemaphoreType.DMA((count,))],
        compiler_params=pltpu.CompilerParams(
            collective_id=0, has_side_effects=True, vmem_limit_bytes=60 * 1024 * 1024
        ),
        cost_estimate=pl.CostEstimate(flops=12 * 10**9, bytes_accessed=24 * 10**6, transcendentals=2 * 10**6),
    )(*[v for v, _ in inputs.values()])
    o = SimpleNamespace(**dict(zip(outs, res)))
    layer = o.o_layer.reshape(rows, H, D)
    x_grad = o.o_x.reshape(rows, H, D)
    if fused:
        return (
            layer, x_grad, o.o_g[:, 0], o.o_q, o.o_k, o.o_v, o.o_out, o.o_g[:, 1], o.o_in, o.o_back, o.o_e.T,
        )

    s = lax.axis_index(SEQ)
    x, c = s // 2, s % 2
    both = (DP, SEQ)

    def scatter(v):
        return lax.psum_scatter(v, both, scatter_dimension=0, tiled=True)

    def rows_back(v, y_first):
        v = v.astype(F32).reshape(2, 2, 2, U, v.shape[-1])
        v = v.transpose(2, 1, 0, 3, 4) if y_first else v.transpose(2, 0, 1, 3, 4)
        return v.reshape(8, U, v.shape[-1])

    def whole(v, y_first):
        v = rows_back(v, y_first)
        full = jnp.zeros((8, 2, U, 2, HC), F32)
        full = lax.dynamic_update_slice(full, v[:, None, :, None, :], (0, x, 0, c, 0))
        return full.reshape(D, 2 * HC)

    wi = jnp.stack([whole(o.wi[f], True) for f in range(NF)], axis=1).reshape(D, FF)
    wo = whole(o.go, False)
    wqkv = [whole(o.gq[:, i * HC : (i + 1) * HC], False) for i in range(3)]
    gains = rows_back(o.gq[:, 3 * HC :], False)
    gfull = lax.dynamic_update_slice(jnp.zeros((8, 2, U, 128), F32), gains[:, None], (0, x, 0, 0)).reshape(D, 128)
    wb = o.wb.astype(F32).reshape(NF * 2, 1, Q, D)
    wb = lax.dynamic_update_slice(jnp.zeros((NF * 2, 4, Q, D), F32), wb, (0, s, 0, 0)).reshape(FF, D)
    ge = o.ge.astype(F32).reshape(2, 2, 2, EB, H).transpose(2, 0, 1, 3, 4).reshape(J, H).T
    return (
        layer, x_grad, scatter(gfull[:, 0]), scatter(wqkv[0]), scatter(wqkv[1]), scatter(wqkv[2]), scatter(wo),
        scatter(gfull[:, 1]), scatter(wi), scatter(wb), lax.psum_scatter(ge, DP, scatter_dimension=1, tiled=True),
    )


def solution(mesh):
    shape = (mesh.shape[DP], mesh.shape[SEQ])
    both = (DP, SEQ)
    in_specs = (
        P(DP, SEQ, None), P(DP, SEQ), P(DP, None), P(SEQ, None),
        P(), P(), P(), P(), P(), P(), P(), P(), P(DP, SEQ, None),
    )
    out_specs = (
        P(DP, SEQ, None), P(DP, SEQ, None), P(both), P(both, None), P(both, None), P(both, None),
        P(both, None), P(both), P(both, None), P(both, None), P(SEQ, DP),
    )
    return jax.shard_map(
        functools.partial(run_layer, shape), mesh=mesh, in_specs=in_specs, out_specs=out_specs, check_vma=False
    )
```

time: 881 us -> 109 us (0.12)
  waiting for transfers between devices: 710 us -> 0 us
  Pallas kernels: 0 us -> 95.7 us
  matrix products: 71.4 us -> 0 us
  blocking collectives: 64.2 us -> 0 us
  between operations: 14.7 us -> 0.7 us
    reduce_scatter x7 -> x0, waiting for transfers between devices: 674 us -> none  [the longest x1 142 us: shards(): lax.psum_scatter(grad_in_w, ('dp', 'seq'), scatter_dimension=0, tiled=True)]
    pallas_call x0 -> x1, Pallas kernels: none -> 95.7 us  [run_layer(): pl.pallas_call(body, out_shape=[jax.ShapeDtypeStruct(sh, dt) for sh, dt i...]
    dot_general x29 -> x0, matrix products: 69.6 us -> none  [the longest x6 19.4 us: contract_rows(): lax.dot_general(left_mat, right_mat, (((0,), (0,)), ((), ())), preferred_...]
    unnamed x1 -> x0, blocking collectives: 39.6 us -> none
    psum x1 -> x0, waiting for transfers between devices: 36 us -> none  [shards(): lax.psum(part_gk.astype(jnp.bfloat16), 'seq').astype(jnp.float32)]
    all_gather x3 -> x0, blocking collectives: 24.6 us -> none  [the longest x1 8.72 us: shards(): key_piece = lax.all_gather(key_rows, 'seq', axis=1, tiled=True)]
  transfers between devices with their start and end apart: 8 -> 0, of which waited for: 7 -> 0; matrix products, arithmetic and copies ran while one was open for 5% -> 0% of each run, Pallas kernels for 0% -> 0%
where the time goes in v1:
time: 109 us; the launch traced here: 108 us
  Pallas kernels  95.7 us (88%)
  local copies, waits for them, and re-layouts  12.1 us (11%)
    pallas_call x1, Pallas kernels, run_layer(): pl.pallas_call(body, out_shape=[jax.ShapeDtypeStruct(sh, dt) for sh, dt i...  95.7 us
    unnamed x23, local copies, waits for them, and re-layouts  8.03 us

profile of v1, /device:TPU:0, one launch (start us, length us, event | category | flops | bytes accessed | tf_op | source)
XLA Modules:
  0.0 108.4 jit_solution(14805530640796925132)
XLA Ops:
  0.6 1.3 %reshape.41.refs_4_ = bf16[1,768]{1,0:T(2,128)(2,1)} reshape(bf16[768]{0:T(1024)(128)(2,1)} %param.20) | data formatting | bytes 3072 | tf_op jit(solution)/shard_map/reshape | solution.py:586
  1.9 1.3 %reshape.42.refs_9_ = bf16[1,768]{1,0:T(2,128)(2,1)} reshape(bf16[768]{0:T(1024)(128)(2,1)} %param.25) | data formatting | bytes 3072 | tf_op jit(solution)/shard_map/reshape | solution.py:591
  3.2 95.7 %shard_map.239 = (bf16[128,768]{1,0:T(8,128)(2,1)}, f32[128,768]{1,0:T(8,128)}, f32[24,128]{1,0:T(8,128)}, f32[24,768]{1,0:T(8,128)}, f32[24,768]{1,0:T(8,128)},...) custom-call(bf16[128,768]{1,0:T(8,128)(2,1)} %bitcast.8, ...), custom_call_target="tpu_custom_call" | custom-call | flops 12000000000 | bytes 24000000 | tf_op jit(solution)/shard_map/pallas_call | solution.py:669
  98.8 0.0 copy-start.5
  98.8 0.0 copy-start.4
  98.9 0.0 copy-start.3
  98.9 0.0 copy-start.2
  98.9 0.0 copy-start.1
  98.9 1.5 %slice_reduce_fusion = (f32[24]{0:T(128)}, f32[24]{0:T(128)}) fusion(f32[24,128]{1,0:T(8,128)} %get-tuple-element.23), kind=kLoop, calls=%fused_computation | loop fusion | bytes 384 | tf_op jit(solution)/shard_map/slice | solution.py:686
  100.4 0.0 copy-start
  100.4 1.7 %copy.36 = bf16[1,128,768]{2,1,0:T(8,128)(2,1)} copy(bf16[1,128,768]{2,1,0:T(8,128)(2,1)} %bitcast.6) | data formatting | bytes 393216
  102.0 0.0 copy-start.6
  102.0 1.8 %copy.37 = f32[1,128,768]{2,1,0:T(8,128)} copy(f32[1,128,768]{2,1,0:T(8,128)} %bitcast.5) | data formatting | bytes 786432
  103.8 0.0 copy-done.5
  103.8 0.6 copy.38
  104.5 0.0 copy-done.4
  104.5 0.6 copy.39
  105.1 0.0 copy-done.3
  105.1 0.6 copy.40
  105.7 0.0 copy-done.2
  105.7 0.6 copy.41
  106.4 0.0 copy-done.1
  106.4 0.7 copy.42
  107.1 0.0 copy-done
  107.1 0.7 copy.43
  107.8 0.0 copy-done.6
  107.8 0.6 copy.44
Async XLA Ops:
  98.8 5.0 %copy-start.5 = (f32[24,768]{1,0:T(8,128)S(1)}, f32[24,768]{1,0:T(8,128)}, u32[]{:S(2)}) copy-start(f32[24,768]{1,0:T(8,128)} %get-tuple-element.47) | copy-start | bytes 221188
  98.8 5.6 %copy-start.4 = (f32[24,768]{1,0:T(8,128)S(1)}, f32[24,768]{1,0:T(8,128)}, u32[]{:S(2)}) copy-start(f32[24,768]{1,0:T(8,128)} %get-tuple-element.48) | copy-start | bytes 221188
  98.9 6.2 %copy-start.3 = (f32[24,768]{1,0:T(8,128)S(1)}, f32[24,768]{1,0:T(8,128)}, u32[]{:S(2)}) copy-start(f32[24,768]{1,0:T(8,128)} %get-tuple-element.49) | copy-start | bytes 221188
  98.9 6.9 %copy-start.2 = (f32[24,768]{1,0:T(8,128)S(1)}, f32[24,768]{1,0:T(8,128)}, u32[]{:S(2)}) copy-start(f32[24,768]{1,0:T(8,128)} %get-tuple-element.50) | copy-start | bytes 221188
  98.9 7.5 %copy-start.1 = (f32[24,3072]{1,0:T(8,128)S(1)}, f32[24,3072]{1,0:T(8,128)}, u32[]{:S(2)}) copy-start(f32[24,3072]{1,0:T(8,128)} %get-tuple-element.52) | copy-start | bytes 884740
  100.4 6.7 %copy-start = (f32[96,768]{1,0:T(8,128)S(1)}, f32[96,768]{1,0:T(8,128)}, u32[]{:S(2)}) copy-start(f32[96,768]{1,0:T(8,128)} %get-tuple-element.53) | copy-start | bytes 884740
  102.0 5.8 %copy-start.6 = (f32[32,128]{1,0:T(8,128)S(1)}, f32[32,128]{1,0:T(8,128)}, u32[]{:S(2)}) copy-start(f32[32,128]{1,0:T(8,128)} %get-tuple-element.30) | copy-start | bytes 49156

commit v2 on v1

v2 whole, which is shorter than its diff:
```python
import functools
from types import SimpleNamespace

import jax
import jax.numpy as jnp
import numpy as np
from jax import lax
from jax.experimental import pallas as pl
from jax.experimental.pallas import tpu as pltpu
from jax.sharding import PartitionSpec as P

HEAD_DIM = 64
DP, SEQ = "dp", "seq"
YLH, LYH = "ylh", "lyh"
BF = jnp.bfloat16
F32 = jnp.float32
MESH = pl.DeviceIdType.MESH
GELU_C = 0.7978845608028654
GELU_K = 0.044715


def nn(a, b):
    return lax.dot_general(a, b, (((1,), (0,)), ((), ())), preferred_element_type=F32)


def tn(a, b):
    return lax.dot_general(a, b, (((0,), (0,)), ((), ())), preferred_element_type=F32)


def nt(a, b):
    return lax.dot_general(a, b, (((1,), (1,)), ((), ())), preferred_element_type=F32)


def selections(d_model, ff):
    unit = d_model // 16
    sel_a = np.zeros((2, d_model // 2, d_model), np.float32)
    for x in range(2):
        for b in range(8):
            j = 4 * (b % 2) + 2 * ((b // 2) % 2) + b // 4
            for o in range(unit):
                sel_a[x, b * unit + o, (2 * j + x) * unit + o] = 1
    q = ff // 32
    sel_c = np.zeros((2, 2, 2 * q, ff // 4), np.float32)
    for x in range(2):
        for c in range(2):
            for y in range(2):
                for o in range(q):
                    sel_c[x, c, y * q + o, (y * 4 + x * 2 + c) * q + o] = 1
    return sel_a, sel_c


def layer_body(fused, r, sl):
    d, s = lax.axis_index(DP), lax.axis_index(SEQ)
    x, c = s // 2, s % 2
    y, lo, hi = d % 2, (d // 2) % 2, d // 4
    to_core = (d, s + 1 - 2 * c)
    to_x = (d, s + 2 - 4 * x)
    to_y = (d + 1 - 2 * y, s)
    to_lo = (d + 2 - 4 * lo, s)
    to_hi = (d + 4 - 8 * hi, s)
    lsem, ssem, rsem = r.lsem, r.ssem, r.rsem
    D = r.h1.shape[1]
    T = r.h1.shape[0]
    H = T // 2
    J = r.sk.shape[0]
    FC = D
    NF = r.w_in.shape[1] // FC
    HC = D // 2
    U = D // 16
    Q = r.wb.shape[2]
    scale = HEAD_DIM ** (-0.5)

    loads = []

    def load(src, dst):
        cp = pltpu.make_async_copy(src, dst, lsem.at[len(loads)])
        loads.append(cp)
        cp.start()
        return cp

    def rc(i, src, dst, dev):
        return pltpu.make_async_remote_copy(
            src_ref=src, dst_ref=dst, send_sem=ssem.at[i], recv_sem=rsem.at[i], device_id=dev, device_id_type=MESH
        )

    l_x = load(r.x_in, r.xb.at[pl.ds(0, H)])
    l_e = load(r.e_in, r.eb.at[pl.ds(0, H)])
    l_wq = load(r.wq_in, r.wq)
    l_wk = load(r.wk_in, r.wk)
    l_wv = load(r.wv_in, r.wv)
    l_dy = load(r.dy_in, r.dyb.at[pl.ds(0, H)])
    l_sa = load(r.sa_in.at[x], r.sa)
    l_wo = load(r.wo_in, r.wo)
    l_sc0 = load(r.sc_in.at[x, c], r.sc.at[pl.ds(0, 2 * Q)])
    l_sc1 = load(r.sc_in.at[x, 1 - c], r.sc.at[pl.ds(2 * Q, 2 * Q)])
    l_w_in = load(r.w_in_in, r.w_in)
    l_w_back = load(r.w_back_in, r.w_back)

    partners = [to_core, to_x] + ([to_y, to_lo, to_hi] if fused else [])
    barrier = pltpu.get_barrier_semaphore()
    for dev in partners:
        pl.semaphore_signal(barrier, inc=1, device_id=dev, device_id_type=MESH)
    r.segf[0] = jnp.broadcast_to(r.seg_in[...].astype(F32), (8, H))
    pl.semaphore_wait(barrier, len(partners))

    x_seg = rc(sl.x_seg, r.segf.at[0], r.segf.at[1], to_x)
    x_e = rc(sl.x_e, r.e_in, r.eb.at[pl.ds(H, H)], to_x)
    x_x = rc(sl.x_x, r.x_in, r.xb.at[pl.ds(H, H)], to_x)
    x_dy = rc(sl.x_dy, r.dy_in, r.dyb.at[pl.ds(H, H)], to_x)
    x_x.start()

    rows_i = lax.broadcasted_iota(jnp.int32, (T, T), 0)
    cols_i = lax.broadcasted_iota(jnp.int32, (T, T), 1)
    eye = jnp.where(rows_i == cols_i, 1.0, 0.0).astype(BF)
    r.eye[...] = eye
    ga = r.ga[...].astype(F32).reshape(1, D)
    gf = r.gf[...].astype(F32).reshape(1, D)
    inv_d = 1.0 / D
    NR = 64

    def norm_rows(v):
        cen = v - jnp.sum(v, axis=1, keepdims=True) * inv_d
        rstd = lax.rsqrt(jnp.sum(cen * cen, axis=1, keepdims=True) * inv_d + 1e-5)
        return cen * rstd, rstd

    def norm_into(src, gain, xh_ref, rs_ref, h_ref, start, count):
        for i in range(start // NR, (start + count) // NR):
            rows = slice(i * NR, (i + 1) * NR)
            xh, rstd = norm_rows(src[rows, :].astype(F32))
            xh_ref[rows, :] = xh
            rs_ref[rows, :] = jnp.broadcast_to(rstd, (NR, 128))
            h_ref[rows, :] = (xh * gain).astype(BF)

    l_x.wait()
    norm_into(r.xb, ga, r.xh1, r.rs1, r.h1, 0, H)
    x_seg.start()
    x_e.start()
    slot_row = r.slot_in[...].astype(F32)
    slot_col = nt(eye, jnp.broadcast_to(slot_row, (T, J)).astype(BF))
    l_wq.wait()
    l_wk.wait()
    l_wv.wait()
    own, far = slice(0, H), slice(H, T)
    r.k[own, :] = nn(r.h1[own, :], r.wk[...]).astype(BF)
    r.v[own, :] = nn(r.h1[own, :], r.wv[...]).astype(BF)
    r.q[own, :] = nn(r.h1[own, :], r.wq[...]).astype(BF)
    l_e.wait()
    l_sa.wait()
    x_x.wait()
    x_dy.start()
    norm_into(r.xb, ga, r.xh1, r.rs1, r.h1, H, H)
    r.k[far, :] = nn(r.h1[far, :], r.wk[...]).astype(BF)

    x_seg.wait()
    x_e.wait()
    seg_row = jnp.concatenate([r.segf[0, 0:1, :], r.segf[1, 0:1, :]], axis=1)
    seg_col = nt(eye, jnp.broadcast_to(seg_row, (J, T)).astype(BF))
    r.sel_t[...] = jnp.where(slot_col == seg_row, 1.0, 0.0)
    r.me[...] = jnp.where(seg_col == slot_row, r.eb[...].astype(F32), 0.0).astype(BF)
    r.met[...] = nt(eye, r.me[...]).astype(BF)

    c_pk = rc(sl.c_pk, r.pk.at[0], r.pkr.at[0], to_core)
    c_pv = rc(sl.c_pv, r.pk.at[1], r.pkr.at[1], to_core)
    r.pk[0] = nn(r.met[...], r.k[...]).astype(BF)
    c_pk.start()
    r.v[far, :] = nn(r.h1[far, :], r.wv[...]).astype(BF)
    r.pk[1] = nn(r.met[...], r.v[...]).astype(BF)
    c_pv.start()
    r.q[far, :] = nn(r.h1[far, :], r.wq[...]).astype(BF)
    r.h1t[0] = nt(r.sa[...], r.h1[...]).astype(BF)
    c_h1t = rc(sl.c_h1t, r.h1t.at[0], r.h1t.at[1], to_core)
    c_pk.wait()
    r.sk[...] = (r.pk[0].astype(F32) + r.pkr[0].astype(F32)).astype(BF)
    c_pv.wait()
    r.sv[...] = (r.pk[1].astype(F32) + r.pkr[1].astype(F32)).astype(BF)
    c_h1t.start()

    lane = lax.broadcasted_iota(jnp.int32, (T, 128), 1)
    head_mask = [jnp.where(lane < 64, 1.0, 0.0).astype(BF), jnp.where(lane < 64, 0.0, 1.0).astype(BF)]

    NP = D // 128

    def fwd_raw(i):
        cols = slice(i * 128, (i + 1) * 128)
        q2 = r.q[:, cols]
        return nt(r.sk[:, cols], jnp.concatenate([q2 * head_mask[0], q2 * head_mask[1]], axis=0))

    def fwd_soft(i, raw):
        for m in range(2 * T // 128):
            h, tc = m * 128 // T, slice(m * 128 % T, m * 128 % T + 128)
            sc = jnp.where(r.sel_t[:, tc] > 0.5, raw[:, m * 128 : (m + 1) * 128] * scale, -1e30)
            e = jnp.exp(sc - jnp.max(sc, axis=0, keepdims=True))
            r.pt[i, h * J : (h + 1) * J, tc] = (e * (1.0 / jnp.sum(e, axis=0, keepdims=True))).astype(BF)

    def fwd_ctx(i):
        cols = slice(i * 128, (i + 1) * 128)
        sv2 = r.sv[:, cols]
        stack = jnp.concatenate([sv2 * head_mask[0], sv2 * head_mask[1]], axis=0)
        r.ctx[:, cols] = tn(r.pt[i], stack).astype(BF)

    raw = fwd_raw(0)
    for i in range(NP):
        nxt = fwd_raw(i + 1) if i + 1 < NP else None
        fwd_soft(i, raw)
        if i > 0:
            fwd_ctx(i - 1)
        raw = nxt
    fwd_ctx(NP - 1)

    l_wo.wait()
    r.mid[...] = r.xb[...].astype(F32) + nn(r.ctx[...], r.wo[...])
    norm_into(r.mid, gf, r.xh2, r.rs2, r.h2, 0, T)
    x_dy.wait()
    l_dy.wait()
    c_dy = rc(sl.c_dy, r.dyb, r.dyo, to_core)
    c_dy.start()
    l_w_in.wait()
    l_w_back.wait()
    l_sc0.wait()
    l_sc1.wait()
    c_h2t = rc(sl.c_h2t, r.h2t.at[0], r.h2t.at[1], to_core)
    c_ctt = rc(sl.c_ctt, r.ctt.at[0], r.ctt.at[1], to_core)

    def c_at(f):
        return rc(sl.c_at + f, r.at.at[f, pl.ds(2 * Q, 2 * Q)], r.atr.at[f], to_core)

    def c_du(f):
        return rc(sl.c_du + f, r.du.at[f, 1 - c], r.dur.at[f], to_core)

    def y_wb(k):
        return rc(sl.y_wb + k, r.wb.at[k, 1 - y], r.wb1.at[k], to_y)

    bits = dict(y=(y, to_y), l=(lo, to_lo), h=(hi, to_hi))

    def span(order, unit, stage):
        start, n = 0, 4 * unit
        for i in range(stage + 1):
            bit = bits[order[i]][0]
            kept, sent = start + bit * n, start + (1 - bit) * n
            if i < stage:
                start, n = kept, n // 2
        return kept, sent, n

    def rows16(start, n):
        return pl.ds(pl.multiple_of(start, 16), n)

    GN = HC + 128
    EB = J // 8
    if fused:
        chain_w = [
            (LYH if k % 2 == 0 else YLH, r.wi.at[k], (r.wi1.at[k], r.wi2.at[k], r.wi3.at[k]), sl.wi + 3 * k, U)
            for k in range(NF)
        ]
        chain_o = (YLH, r.go, (r.go1, r.go2, r.go3), sl.go, U)
        chain_q = (LYH, r.gq, (r.gq1, r.gq2, r.gq3), sl.gq, U)
        chain_k = (YLH, r.gk, (r.gk1, r.gk2, r.gk3), sl.gk, U)
        chain_v = (YLH, r.gv, (r.gv1, r.gv2, r.gv3), sl.gv, U)
        chain_e = (LYH, r.ge, (r.ge1, r.ge2, r.ge3), sl.ge, EB)

    def add_into(dst, idx, src):
        dst[idx] = (dst[idx].astype(F32) + src.astype(F32)).astype(BF)

    def lo_wb(p):
        return rc(sl.lo_wb + p, r.wb.at[2 * p + 1 - lo, y], r.wb2.at[p], to_lo)

    def hi_wb():
        return rc(sl.hi_wb, r.wb.at[2 * (1 - hi) + lo, y], r.wb3, to_hi)

    def pump_wb(k):
        if k < 4:
            y_wb(k).wait()
            add_into(r.wb, (k, y), r.wb1[k])

            @pl.when(lo == 1 - k % 2)
            def _():
                lo_wb(k // 2).start()
        else:
            p = k - 4
            lo_wb(p).wait()
            add_into(r.wb, (2 * p + lo, y), r.wb2[p])

            @pl.when(hi == 1 - p)
            def _():
                hi_wb().start()

    def pump(steps):
        for step in steps:
            if step[0] is None:
                pump_wb(step[1])
            else:
                st_next(step[0], step[1])

    def st_copy(chain, stage):
        order, buf, got, slot, unit = chain
        _, sent, n = span(order, unit, stage)
        return rc(slot + stage, buf.at[rows16(sent, n)], got[stage], bits[order[stage]][1])

    def st_next(chain, stage):
        order, buf, got, _, unit = chain
        st_copy(chain, stage).wait()
        kept, _, n = span(order, unit, stage)
        add_into(buf, (rows16(kept, n), slice(None)), got[stage][...])
        st_copy(chain, stage + 1).start()

    def st_last(chain):
        order, buf, got, _, unit = chain
        st_copy(chain, 2).wait()
        kept, _, n = span(order, unit, 2)
        return buf[rows16(kept, n), :].astype(F32) + got[2][...].astype(F32)

    def swap_rows(buf, cols, val, unit):
        q = 2 * unit
        for b in range(4):
            to = (b % 2) * 2 + b // 2
            buf[to * q : (to + 1) * q, cols] = val[b * q : (b + 1) * q, :].astype(BF)

    SB = 256
    GR = 32

    if fused:
        b0, b1, b2, b3, b4, b5 = [(None, k) for k in range(6)]
        w0, w1, w2, w3 = chain_w
        FFN_PUMPS = [[], [], [b0], [(w0, 0)]]
        MID_PUMPS = [[b1], [(w1, 0)]]
        ATT_PUMPS = [[], [b2, b4], [(w0, 1)], [(w2, 0)], [], [b3]]
        END_PUMPS = [(w1, 1), (w2, 1), (w3, 0), b5, (chain_q, 0), (chain_e, 0), (w3, 1), (chain_o, 0), (chain_q, 1),
                     (chain_e, 1), (chain_o, 1), (chain_k, 0), (chain_v, 0), (chain_k, 1), (chain_v, 1)]

    def swapped(buf, val, order, unit):
        if order == YLH:
            buf[...] = val.astype(BF)
        else:
            swap_rows(buf, slice(0, val.shape[1]), val, unit)

    def grad_wi(k):
        c_du(k).wait()
        val = nn(r.h2t[0], r.du[k, c]) + nn(r.h2t[1], r.dur[k])
        if not fused:
            r.wi[k] = val.astype(BF)
            return
        swapped(chain_w[k][1], val, chain_w[k][0], U)
        st_copy(chain_w[k], 0).start()

    for k in range(NF):
        for b in range(FC // SB):
            off = k * FC + b * SB
            u = nn(r.h2[...], r.w_in[:, off : off + SB])
            g = nt(r.dyb[...], r.w_back[off : off + SB, :])
            for m in range(T // GR):
                rr = slice(m * GR, (m + 1) * GR)
                um = u[rr, :]
                u2 = um * um
                th = jnp.tanh(um * (GELU_C + (GELU_C * GELU_K) * u2))
                half = 0.5 + 0.5 * th
                r.a[rr, b * SB : (b + 1) * SB] = (um * half).astype(BF)
                slope = half + (um * half) * ((1.0 - th) * (GELU_C + (3.0 * GELU_C * GELU_K) * u2))
                r.duf[rr, b * SB : (b + 1) * SB] = (slope * g[rr, :]).astype(BF)
        r.at[k] = nt(r.sc[...], r.a[...]).astype(BF)
        c_at(k).start()
        r.du[k, 0] = r.duf[:, 0:HC]
        r.du[k, 1] = r.duf[:, HC : 2 * HC]
        c_du(k).start()
        if k == 0:
            r.h2t[0] = nt(r.sa[...], r.h2[...]).astype(BF)
            c_h2t.start()
            c_dy.wait()
        if k == 1:
            c_h2t.wait()
        if k > 0:
            grad_wi(k - 1)
        else:
            r.ctt[0] = nt(r.sa[...], r.ctx[...]).astype(BF)
            c_ctt.start()
        c_at(k).wait()
        wb = nn(r.at[k, 0 : 2 * Q, :], r.dyb[...]) + nn(r.atr[k], r.dyo[...])
        r.wb[k, 0] = wb[0:Q, :].astype(BF)
        r.wb[k, 1] = wb[Q : 2 * Q, :].astype(BF)
        if fused:
            y_wb(k).start()
        rows = slice(k * FC, (k + 1) * FC)
        part_d = nt(r.duf[...], r.w_in[:, rows])
        part_o = nn(r.a[0:H, :], r.w_back[rows, :])
        if k == 0:
            r.oacc[...] = part_o
            r.dacc[...] = part_d
        else:
            r.oacc[...] += part_o
            r.dacc[...] += part_d
        if fused:
            pump(FFN_PUMPS[k])
    grad_wi(NF - 1)

    if fused:
        pump(MID_PUMPS[0])
    gsum = None
    for i in range(T // NR):
        rows = slice(i * NR, (i + 1) * NR)
        dn, xh = r.dacc[rows, :], r.xh2[rows, :]
        part = jnp.sum(dn * xh, axis=0, keepdims=True)
        gsum = part if gsum is None else gsum + part
        dg = dn * gf
        m1 = jnp.sum(dg, axis=1, keepdims=True) * inv_d
        m2 = jnp.sum(dg * xh, axis=1, keepdims=True) * inv_d
        dmid = r.dyb[rows, :].astype(F32) + r.rs2[rows, 0:1] * (dg - m1 - xh * m2)
        r.dmid[rows, :] = dmid
        b = dmid.astype(BF)
        r.dmb[0, rows, :] = b[:, 0:HC]
        r.dmb[1, rows, :] = b[:, HC : 2 * HC]
    r.gvec[1:2, :] = gsum
    c_dm = rc(sl.c_dm, r.dmb.at[1 - c], r.dmr, to_core)
    c_dm.start()
    r.dctx[...] = (nt(r.dmb[0], r.wo[:, 0:HC]) + nt(r.dmb[1], r.wo[:, HC : 2 * HC])).astype(BF)
    r.o_layer[...] = (r.mid[0:H, :] + r.oacc[...]).astype(BF)
    if fused:
        pump(MID_PUMPS[1])

    def c_ds(i):
        return rc(sl.c_ds + i, r.pd.at[i], r.pdr.at[i], to_core)

    def bwd_dp(i):
        cols = slice(i * 128, (i + 1) * 128)
        dc2 = r.dctx[:, cols]
        return nt(r.sv[:, cols], jnp.concatenate([dc2 * head_mask[0], dc2 * head_mask[1]], axis=0))

    def bwd_soft(i, dpf):
        for m in range(2 * T // 128):
            h, tc = m * 128 // T, slice(m * 128 % T, m * 128 % T + 128)
            pf = r.pt[i, h * J : (h + 1) * J, tc].astype(F32)
            dp = dpf[:, m * 128 : (m + 1) * 128]
            ds = pf * (dp - jnp.sum(pf * dp, axis=0, keepdims=True))
            r.draw[i % 2, h * J : (h + 1) * J, tc] = (ds * scale).astype(BF)

    def bwd_out(i):
        cols = slice(i * 128, (i + 1) * 128)
        q2, dc2, sk2 = r.q[:, cols], r.dctx[:, cols], r.sk[:, cols]
        draw = r.draw[i % 2]
        dsv = nn(r.pt[i, 0:J], dc2 * head_mask[0]) + nn(r.pt[i, J : 2 * J], dc2 * head_mask[1])
        dsk = nn(draw[0:J], q2 * head_mask[0]) + nn(draw[J : 2 * J], q2 * head_mask[1])
        r.pd[i, 0] = dsk.astype(BF)
        r.pd[i, 1] = dsv.astype(BF)
        c_ds(i).start()
        stack = jnp.concatenate([sk2 * head_mask[0], sk2 * head_mask[1]], axis=0)
        r.dqkv[0, i // 3, :, (i % 3) * 128 : (i % 3 + 1) * 128] = tn(draw, stack).astype(BF)

    dpf = bwd_dp(0)
    for i in range(NP):
        nxt = bwd_dp(i + 1) if i + 1 < NP else None
        bwd_soft(i, dpf)
        if i > 0:
            bwd_out(i - 1)
        dpf = nxt
        if i == 0:
            c_ctt.wait()
            c_dm.wait()
            r.go[...] = (nn(r.ctt[0], r.dmb[c]) + nn(r.ctt[1], r.dmr[...])).astype(BF)
            if fused:
                st_copy(chain_o, 0).start()
        if fused:
            pump(ATT_PUMPS[i])
    bwd_out(NP - 1)

    def c_g(i):
        return rc(sl.c_g + i, r.dqkv.at[i, 1 - c], r.dqr.at[i], to_core)

    c_g(0).start()
    for i in range(D // 128):
        cols = slice(i * 128, (i + 1) * 128)
        c_ds(i).wait()
        r.dsk[:, cols] = (r.pd[i, 0].astype(F32) + r.pdr[i, 0].astype(F32)).astype(BF)
        r.dsv[:, cols] = (r.pd[i, 1].astype(F32) + r.pdr[i, 1].astype(F32)).astype(BF)

    dk = nn(r.me[...], r.dsk[...]).astype(BF)
    r.dqkv[1, 0] = dk[:, 0:HC]
    r.dqkv[1, 1] = dk[:, HC : 2 * HC]
    c_g(1).start()
    dv = nn(r.me[...], r.dsv[...]).astype(BF)
    r.dqkv[2, 0] = dv[:, 0:HC]
    r.dqkv[2, 1] = dv[:, HC : 2 * HC]
    c_g(2).start()

    def wgrad(i):
        c_g(i).wait()
        return nn(r.h1t[0], r.dqkv[i, c]) + nn(r.h1t[1], r.dqr[i])

    c_h1t.wait()
    swap_rows(r.gq, slice(0, HC), wgrad(0), U)
    if fused:
        st_copy(chain_q, 0).start()
    r.gk[...] = wgrad(1).astype(BF)
    if fused:
        st_copy(chain_k, 0).start()
    r.gv[:, 0:HC] = wgrad(2).astype(BF)

    acc = None
    for i, w in enumerate((r.wq, r.wk, r.wv)):
        for hf in range(2):
            part = nt(r.dqkv[i, hf], w[:, hf * HC : (hf + 1) * HC])
            acc = part if acc is None else acc + part
    r.dacc[...] = acc

    gsum = None
    for i in range(T // NR):
        rows = slice(i * NR, (i + 1) * NR)
        dn, xh = r.dacc[rows, :], r.xh1[rows, :]
        part = jnp.sum(dn * xh, axis=0, keepdims=True)
        gsum = part if gsum is None else gsum + part
        if i < H // NR:
            dg = dn * ga
            m1 = jnp.sum(dg, axis=1, keepdims=True) * inv_d
            m2 = jnp.sum(dg * xh, axis=1, keepdims=True) * inv_d
            r.o_x[rows, :] = r.dmid[rows, :] + r.rs1[rows, 0:1] * (dg - m1 - xh * m2)
    r.gvec[0:1, :] = gsum
    gains = jnp.concatenate([r.gvec[0:2, :], jnp.zeros((126, D), F32)], axis=0).astype(BF)
    r.gv[:, HC:GN] = nt(r.sa[...], gains).astype(BF)
    if fused:
        st_copy(chain_v, 0).start()

    de = nt(r.dsk[...], r.k[0:H, :]) + nt(r.dsv[...], r.v[0:H, :])
    de = jnp.where(r.sel_t[:, 0:H] > 0.5, de, 0.0).astype(BF)
    for b in range(8):
        b2, b1, b0 = b // 4, (b // 2) % 2, b % 2
        j = 4 * b0 + 2 * b2 + b1
        r.ge[b * EB : (b + 1) * EB, :] = de[j * EB : (j + 1) * EB, :]

    if not fused:
        return

    st_copy(chain_e, 0).start()
    pump(END_PUMPS)

    fin = r.fin
    for k in range(NF):
        fin[:, k * HC : (k + 1) * HC] = st_last(chain_w[k])
    at = NF * HC
    for chain in (chain_o, chain_q, chain_v, chain_k):
        width = chain[1].shape[1]
        fin[:, at : at + width] = st_last(chain)
        at += width
    half = U // 2
    c_fin = rc(sl.c_fin, fin.at[pl.ds(pl.multiple_of((1 - c) * half, 8), half)], r.finr, to_core)
    c_fin.start()
    hi_wb().wait()
    r.o_back[...] = r.wb[2 * hi + lo, y].astype(F32) + r.wb3[...].astype(F32)
    r.o_e[...] = st_last(chain_e)
    c_fin.wait()
    mine = pl.ds(pl.multiple_of(c * half, 8), half)

    def put(dst, base, src_col):
        dst[:, pl.ds(pl.multiple_of(base + c * HC, 128), HC)] = fin[mine, src_col : src_col + HC]
        dst[:, pl.ds(pl.multiple_of(base + (1 - c) * HC, 128), HC)] = r.finr[:, src_col : src_col + HC]

    for k in range(NF):
        put(r.o_in, k * FC, k * HC)
    for dst, at in ((r.o_out, NF * HC), (r.o_q, (NF + 1) * HC), (r.o_v, (NF + 2) * HC), (r.o_k, (NF + 2) * HC + GN)):
        put(dst, 0, at)
    at = (NF + 3) * HC
    r.o_g[...] = fin[mine, at : at + 128] + r.finr[:, at : at + 128]


def hand_over(r, names):
    copies = []
    for i, (src, dst) in enumerate(names):
        cp = pltpu.make_async_copy(src, dst, r.sem.at[i])
        cp.start()
        copies.append(cp)
    g = jnp.concatenate([r.s_g[...], jnp.zeros((128 - r.s_g.shape[0], 128), F32)], axis=0).T
    n = r.s_g.shape[0]
    r.d_ga[...] = g[0, 0:n]
    r.d_gf[...] = g[1, 0:n]
    for cp in copies:
        cp.wait()


def run_layer(mesh_shape, tokens, seg_ids, slot_doc, proj_e, g_attn, w_query, w_key, w_value, w_out, g_ffn, w_in,
              w_back, cotangent):
    n_dp, n_seq = mesh_shape
    rows, H, D = tokens.shape
    J = proj_e.shape[1]
    FF = w_in.shape[1]
    fused = n_dp == 8
    T = 2 * H
    HC, U, NF, Q = D // 2, D // 16, FF // D, FF // 32
    EB = J // 8
    GN = HC + 128
    sel_a, sel_c = (jnp.asarray(m, BF) for m in selections(D, FF))

    inputs = dict(
        x_in=(tokens.reshape(H, D), False),
        seg_in=(seg_ids.reshape(1, H), True),
        slot_in=(slot_doc.reshape(1, J), True),
        e_in=(proj_e, False),
        ga=(g_attn, True),
        wq_in=(w_query, False),
        wk_in=(w_key, False),
        wv_in=(w_value, False),
        wo_in=(w_out, False),
        gf=(g_ffn, True),
        w_in_in=(w_in, False),
        w_back_in=(w_back, False),
        dy_in=(cotangent.reshape(H, D), False),
        sa_in=(sel_a, False),
        sc_in=(sel_c, False),
    )
    parts = dict(
        wb=((NF, 2, Q, D), BF),
        wi=((NF, D // 2, HC), BF),
        go=((D // 2, HC), BF),
        gq=((D // 2, HC), BF),
        gk=((D // 2, HC), BF),
        gv=((D // 2, GN), BF),
        ge=((J, H), BF),
    )
    outs = dict(o_layer=((H, D), BF), o_x=((H, D), F32))
    if fused:
        outs.update(
            o_g=((U // 2, 128), F32),
            o_q=((U // 2, D), F32),
            o_k=((U // 2, D), F32),
            o_v=((U // 2, D), F32),
            o_out=((U // 2, D), F32),
            o_in=((U // 2, FF), F32),
            o_back=((Q, D), F32),
            o_e=((EB, H), F32),
        )
    else:
        outs.update(parts)
    scratch = dict(
        xb=((T, D), BF), eb=((T, J), BF), segf=((2, 8, H), F32),
        wq=((D, D), BF), wk=((D, D), BF), wv=((D, D), BF), wo=((D, D), BF),
        w_in=((D, FF), BF), w_back=((FF, D), BF),
        dyb=((T, D), BF), dyo=((T, D), BF),
        sa=((D // 2, D), BF), sc=((4 * Q, FF // 4), BF),
        eye=((T, T), BF),
        h1=((T, D), BF), xh1=((T, D), F32), rs1=((T, 128), F32),
        q=((T, D), BF), k=((T, D), BF), v=((T, D), BF),
        sel_t=((J, T), F32), me=((T, J), BF), met=((J, T), BF),
        pk=((2, J, D), BF), pkr=((2, J, D), BF), sk=((J, D), BF), sv=((J, D), BF),

        pt=((D // 128, 2 * J, T), BF), ctx=((T, D), BF),
        mid=((T, D), F32), xh2=((T, D), F32), rs2=((T, 128), F32), h2=((T, D), BF),
        h1t=((2, D // 2, T), BF), h2t=((2, D // 2, T), BF), ctt=((2, D // 2, T), BF),
        a=((T, D), BF), duf=((T, D), BF), du=((NF, 2, T, HC), BF), dur=((NF, T, HC), BF),
        at=((NF, 4 * Q, T), BF), atr=((NF, 2 * Q, T), BF),
        oacc=((H, D), F32), dacc=((T, D), F32), dmid=((T, D), F32), gvec=((8, D), F32),
        dmb=((2, T, HC), BF), dmr=((T, HC), BF), dctx=((T, D), BF), draw=((2, 2 * J, T), BF),
        pd=((D // 128, 2, J, 128), BF), pdr=((D // 128, 2, J, 128), BF),
        dsk=((J, D), BF), dsv=((J, D), BF),
        dqkv=((3, 2, T, HC), BF), dqr=((3, T, HC), BF),
    )
    if fused:
        scratch.update(
            parts,
            wb1=((NF, Q, D), BF), wb2=((2, Q, D), BF), wb3=((Q, D), BF),
            wi1=((NF, 4 * U, HC), BF), wi2=((NF, 2 * U, HC), BF), wi3=((NF, U, HC), BF),
            go1=((4 * U, HC), BF), go2=((2 * U, HC), BF), go3=((U, HC), BF),
            gq1=((4 * U, HC), BF), gq2=((2 * U, HC), BF), gq3=((U, HC), BF),
            gk1=((4 * U, HC), BF), gk2=((2 * U, HC), BF), gk3=((U, HC), BF),
            gv1=((4 * U, GN), BF), gv2=((2 * U, GN), BF), gv3=((U, GN), BF),
            ge1=((4 * EB, H), BF), ge2=((2 * EB, H), BF), ge3=((EB, H), BF),
            fin=((U, NF * HC + 3 * HC + GN), F32), finr=((U // 2, NF * HC + 3 * HC + GN), F32),
        )
    counts = dict(
        x_seg=1, x_e=1, x_x=1, x_dy=1, c_pk=1, c_pv=1, c_h1t=1, c_h2t=1, c_dy=1, c_ctt=1, c_at=NF, c_du=NF, c_dm=1,
        c_ds=D // 128, c_g=3, y_wb=NF, wi=3 * NF, lo_wb=2, hi_wb=1, go=3, gq=3, gk=3, gv=3, ge=3, c_fin=1,
    )
    sl, count = SimpleNamespace(), 0
    for name, n in counts.items():
        setattr(sl, name, count)
        count += n
    names = [*inputs, *outs, *scratch]

    def body(*refs):
        r = SimpleNamespace(**dict(zip(names, refs)))
        r.lsem, r.ssem, r.rsem = refs[len(names) :]
        layer_body(fused, r, sl)

    res = pl.pallas_call(
        body,
        out_shape=[jax.ShapeDtypeStruct(sh, dt) for sh, dt in outs.values()],
        in_specs=[pl.BlockSpec(memory_space=pltpu.VMEM if v else pl.ANY) for _, v in inputs.values()],
        out_specs=[pl.BlockSpec(memory_space=pltpu.VMEM) for _ in outs],
        scratch_shapes=[pltpu.VMEM(sh, dt) for sh, dt in scratch.values()]
        + [pltpu.SemaphoreType.DMA((12,)), pltpu.SemaphoreType.DMA((count,)), pltpu.SemaphoreType.DMA((count,))],
        compiler_params=pltpu.CompilerParams(
            collective_id=0, has_side_effects=True, vmem_limit_bytes=60 * 1024 * 1024
        ),
        cost_estimate=pl.CostEstimate(flops=12 * 10**9, bytes_accessed=24 * 10**6, transcendentals=2 * 10**6),
    )(*[v for v, _ in inputs.values()])
    o = SimpleNamespace(**dict(zip(outs, res)))
    if fused:
        src = dict(s_layer=o.o_layer, s_x=o.o_x, s_q=o.o_q, s_k=o.o_k, s_v=o.o_v, s_out=o.o_out, s_in=o.o_in,
                   s_back=o.o_back, s_e=o.o_e, s_g=o.o_g)
        n_copy = len(src) - 1
        dst = dict(
            d_layer=((rows, H, D), BF), d_x=((rows, H, D), F32), d_q=((U // 2, D), F32), d_k=((U // 2, D), F32),
            d_v=((U // 2, D), F32), d_out=((U // 2, D), F32), d_in=((U // 2, FF), F32), d_back=((Q, D), F32),
            d_e=((EB, H), F32), d_ga=((U // 2,), F32), d_gf=((U // 2,), F32),
        )

        def tail(*refs):
            r = SimpleNamespace(**dict(zip([*src, *dst], refs)))
            r.sem = refs[-1]
            r.d_layer, r.d_x = r.d_layer.at[0], r.d_x.at[0]
            pairs = list(zip(vars(r).values(), list(vars(r).values())[len(src) :]))[:n_copy]
            hand_over(r, pairs)

        res = pl.pallas_call(
            tail,
            out_shape=[jax.ShapeDtypeStruct(sh, dt) for sh, dt in dst.values()],
            in_specs=[pl.BlockSpec(memory_space=pl.ANY)] * n_copy + [pl.BlockSpec(memory_space=pltpu.VMEM)],
            out_specs=[pl.BlockSpec(memory_space=pltpu.VMEM)] * len(dst),
            scratch_shapes=[pltpu.SemaphoreType.DMA((n_copy,))],
        )(*src.values())
        o = SimpleNamespace(**dict(zip(dst, res)))
        return o.d_layer, o.d_x, o.d_ga, o.d_q, o.d_k, o.d_v, o.d_out, o.d_gf, o.d_in, o.d_back, o.d_e.T

    layer = o.o_layer.reshape(rows, H, D)
    x_grad = o.o_x.reshape(rows, H, D)

    s = lax.axis_index(SEQ)
    x, c = s // 2, s % 2
    both = (DP, SEQ)

    def scatter(v):
        return lax.psum_scatter(v, both, scatter_dimension=0, tiled=True)

    def rows_back(v, y_first):
        v = v.astype(F32).reshape(2, 2, 2, U, v.shape[-1])
        v = v.transpose(2, 1, 0, 3, 4) if y_first else v.transpose(2, 0, 1, 3, 4)
        return v.reshape(8, U, v.shape[-1])

    def whole(v, y_first):
        v = rows_back(v, y_first)
        full = jnp.zeros((8, 2, U, 2, HC), F32)
        full = lax.dynamic_update_slice(full, v[:, None, :, None, :], (0, x, 0, c, 0))
        return full.reshape(D, 2 * HC)

    wi = jnp.stack([whole(o.wi[f], True) for f in range(NF)], axis=1).reshape(D, FF)
    wo = whole(o.go, True)
    wqkv = [whole(o.gq, False), whole(o.gk, True), whole(o.gv[:, :HC], True)]
    gains = rows_back(o.gv[:, HC:], True)
    gfull = lax.dynamic_update_slice(jnp.zeros((8, 2, U, 128), F32), gains[:, None], (0, x, 0, 0)).reshape(D, 128)
    wb = o.wb.astype(F32).reshape(NF * 2, 1, Q, D)
    wb = lax.dynamic_update_slice(jnp.zeros((NF * 2, 4, Q, D), F32), wb, (0, s, 0, 0)).reshape(FF, D)
    ge = o.ge.astype(F32).reshape(2, 2, 2, EB, H).transpose(2, 0, 1, 3, 4).reshape(J, H).T
    return (
        layer, x_grad, scatter(gfull[:, 0]), scatter(wqkv[0]), scatter(wqkv[1]), scatter(wqkv[2]), scatter(wo),
        scatter(gfull[:, 1]), scatter(wi), scatter(wb), lax.psum_scatter(ge, DP, scatter_dimension=1, tiled=True),
    )


def solution(mesh):
    shape = (mesh.shape[DP], mesh.shape[SEQ])
    both = (DP, SEQ)
    in_specs = (
        P(DP, SEQ, None), P(DP, SEQ), P(DP, None), P(SEQ, None),
        P(), P(), P(), P(), P(), P(), P(), P(), P(DP, SEQ, None),
    )
    out_specs = (
        P(DP, SEQ, None), P(DP, SEQ, None), P(both), P(both, None), P(both, None), P(both, None),
        P(both, None), P(both), P(both, None), P(both, None), P(SEQ, DP),
    )
    return jax.shard_map(
        functools.partial(run_layer, shape), mesh=mesh, in_specs=in_specs, out_specs=out_specs, check_vma=False
    )
```

time: 109 us -> 81.3 us (0.75)
  Pallas kernels: 95.7 us -> 80.2 us
  local copies, waits for them, and re-layouts: 12.1 us -> 0 us
    pallas_call x1, Pallas kernels: 95.7 us -> 77 us  [run_layer(): pl.pallas_call(body, out_shape=[jax.ShapeDtypeStruct(sh, dt) for sh, dt i...]
    unnamed x23 -> x0, local copies, waits for them, and re-layouts: 8.03 us -> none
    pallas_call x0 -> x1, Pallas kernels: none -> 3.27 us  [run_layer(): pl.pallas_call(tail, out_shape=[jax.ShapeDtypeStruct(sh, dt) for sh, dt i...]
    reshape x2 -> x0, local copies, waits for them, and re-layouts: 2.52 us -> none  [the longest x1 1.26 us: run_layer(): g_attn.reshape(1, D)]
    slice x1 -> x0, local copies, waits for them, and re-layouts: 1.5 us -> none  [run_layer(): o.o_g[:, 1]]
where the time goes in v2:
time: 81.3 us; the launch traced here: 81.1 us
  Pallas kernels  80.2 us (99%)
  between operations  0.82 us (1%)
    pallas_call x1, Pallas kernels, run_layer(): pl.pallas_call(body, out_shape=[jax.ShapeDtypeStruct(sh, dt) for sh, dt i...  77 us
    pallas_call x1, Pallas kernels, run_layer(): pl.pallas_call(tail, out_shape=[jax.ShapeDtypeStruct(sh, dt) for sh, dt i...  3.27 us

profile of v2, /device:TPU:0, one launch (start us, length us, event | category | flops | bytes accessed | tf_op | source)
XLA Modules:
  0.0 81.1 jit_solution(5581708575217246879)
XLA Ops:
  0.6 77.0 %shard_map.230 = (bf16[128,768]{1,0:T(8,128)(2,1)}, f32[128,768]{1,0:T(8,128)}, f32[24,128]{1,0:T(8,128)}, f32[24,768]{1,0:T(8,128)}, f32[24,768]{1,0:T(8,128)},...) custom-call(bf16[128,768]{1,0:T(8,128)(2,1)} %bitcast.3, ...), custom_call_target="tpu_custom_call" | custom-call | flops 12000000000 | bytes 24000000 | tf_op jit(solution)/shard_map/pallas_call | solution.py:677
  77.6 3.3 %shard_map.231 = (bf16[1,128,768]{2,1,0:T(8,128)(2,1)}, f32[1,128,768]{2,1,0:T(8,128)}, f32[24,768]{1,0:T(8,128)}, f32[24,768]{1,0:T(8,128)}, f32[24,768]{1,0:T(...) custom-call(bf16[128,768]{1,0:T(8,128)(2,1)} %get-tuple-element.32.r, ...), custom_call_target="tpu_custom_call" | custom-call | tf_op jit(solution)/shard_map/pallas_call | solution.py:707

commit v3 on v2

--- a/solution.py
+++ b/solution.py
@@ -83,7 +83,13 @@
             src_ref=src, dst_ref=dst, send_sem=ssem.at[i], recv_sem=rsem.at[i], device_id=dev, device_id_type=MESH
         )
 
+    partners = [to_core, to_x] + ([to_y, to_lo, to_hi] if fused else [])
+    barrier = pltpu.get_barrier_semaphore()
+    for dev in partners:
+        pl.semaphore_signal(barrier, inc=1, device_id=dev, device_id_type=MESH)
     l_x = load(r.x_in, r.xb.at[pl.ds(0, H)])
+    l_seg = load(r.seg_in, r.segs.at[0])
+    l_slot = load(r.slot_in, r.slot)
     l_e = load(r.e_in, r.eb.at[pl.ds(0, H)])
     l_wq = load(r.wq_in, r.wq)
     l_wk = load(r.wk_in, r.wk)
@@ -96,14 +102,9 @@
     l_w_in = load(r.w_in_in, r.w_in)
     l_w_back = load(r.w_back_in, r.w_back)
 
-    partners = [to_core, to_x] + ([to_y, to_lo, to_hi] if fused else [])
-    barrier = pltpu.get_barrier_semaphore()
-    for dev in partners:
-        pl.semaphore_signal(barrier, inc=1, device_id=dev, device_id_type=MESH)
-    r.segf[0] = jnp.broadcast_to(r.seg_in[...].astype(F32), (8, H))
     pl.semaphore_wait(barrier, len(partners))
 
-    x_seg = rc(sl.x_seg, r.segf.at[0], r.segf.at[1], to_x)
+    x_seg = rc(sl.x_seg, r.seg_in, r.segs.at[1], to_x)
     x_e = rc(sl.x_e, r.e_in, r.eb.at[pl.ds(H, H)], to_x)
     x_x = rc(sl.x_x, r.x_in, r.xb.at[pl.ds(H, H)], to_x)
     x_dy = rc(sl.x_dy, r.dy_in, r.dyb.at[pl.ds(H, H)], to_x)
@@ -135,7 +136,8 @@
     norm_into(r.xb, ga, r.xh1, r.rs1, r.h1, 0, H)
     x_seg.start()
     x_e.start()
-    slot_row = r.slot_in[...].astype(F32)
+    l_slot.wait()
+    slot_row = r.slot[...].astype(F32)
     slot_col = nt(eye, jnp.broadcast_to(slot_row, (T, J)).astype(BF))
     l_wq.wait()
     l_wk.wait()
@@ -153,7 +155,8 @@
 
     x_seg.wait()
     x_e.wait()
-    seg_row = jnp.concatenate([r.segf[0, 0:1, :], r.segf[1, 0:1, :]], axis=1)
+    l_seg.wait()
+    seg_row = jnp.concatenate([r.segs[0], r.segs[1]], axis=1).astype(F32)
     seg_col = nt(eye, jnp.broadcast_to(seg_row, (J, T)).astype(BF))
     r.sel_t[...] = jnp.where(slot_col == seg_row, 1.0, 0.0)
     r.me[...] = jnp.where(seg_col == slot_row, r.eb[...].astype(F32), 0.0).astype(BF)
@@ -167,13 +170,7 @@
     r.pk[1] = nn(r.met[...], r.v[...]).astype(BF)
     c_pv.start()
     r.q[far, :] = nn(r.h1[far, :], r.wq[...]).astype(BF)
-    r.h1t[0] = nt(r.sa[...], r.h1[...]).astype(BF)
     c_h1t = rc(sl.c_h1t, r.h1t.at[0], r.h1t.at[1], to_core)
-    c_pk.wait()
-    r.sk[...] = (r.pk[0].astype(F32) + r.pkr[0].astype(F32)).astype(BF)
-    c_pv.wait()
-    r.sv[...] = (r.pk[1].astype(F32) + r.pkr[1].astype(F32)).astype(BF)
-    c_h1t.start()
 
     lane = lax.broadcasted_iota(jnp.int32, (T, 128), 1)
     head_mask = [jnp.where(lane < 64, 1.0, 0.0).astype(BF), jnp.where(lane < 64, 0.0, 1.0).astype(BF)]
@@ -198,10 +195,15 @@
         stack = jnp.concatenate([sv2 * head_mask[0], sv2 * head_mask[1]], axis=0)
         r.ctx[:, cols] = tn(r.pt[i], stack).astype(BF)
 
+    c_pk.wait()
+    r.sk[...] = (r.pk[0].astype(F32) + r.pkr[0].astype(F32)).astype(BF)
     raw = fwd_raw(0)
     for i in range(NP):
         nxt = fwd_raw(i + 1) if i + 1 < NP else None
         fwd_soft(i, raw)
+        if i == 0:
+            c_pv.wait()
+            r.sv[...] = (r.pk[1].astype(F32) + r.pkr[1].astype(F32)).astype(BF)
         if i > 0:
             fwd_ctx(i - 1)
         raw = nxt
@@ -245,16 +247,18 @@
         return pl.ds(pl.multiple_of(start, 16), n)
 
     GN = HC + 128
+    VW = GN // 2
     EB = J // 8
     if fused:
         chain_w = [
-            (LYH if k % 2 == 0 else YLH, r.wi.at[k], (r.wi1.at[k], r.wi2.at[k], r.wi3.at[k]), sl.wi + 3 * k, U)
+            (LYH, r.wi.at[k], (r.wi1.at[k], r.wi2.at[k], r.wi3.at[k]), sl.wi + 3 * k, U)
             for k in range(NF)
         ]
         chain_o = (YLH, r.go, (r.go1, r.go2, r.go3), sl.go, U)
-        chain_q = (LYH, r.gq, (r.gq1, r.gq2, r.gq3), sl.gq, U)
+        chain_q = (YLH, r.gq, (r.gq1, r.gq2, r.gq3), sl.gq, U)
         chain_k = (YLH, r.gk, (r.gk1, r.gk2, r.gk3), sl.gk, U)
-        chain_v = (YLH, r.gv, (r.gv1, r.gv2, r.gv3), sl.gv, U)
+        chain_va = (YLH, r.gva, (r.gva1, r.gva2, r.gva3), sl.gva, U)
+        chain_vb = (YLH, r.gvb, (r.gvb1, r.gvb2, r.gvb3), sl.gvb, U)
         chain_e = (LYH, r.ge, (r.ge1, r.ge2, r.ge3), sl.ge, EB)
 
     def add_into(dst, idx, src):
@@ -320,11 +324,12 @@
     if fused:
         b0, b1, b2, b3, b4, b5 = [(None, k) for k in range(6)]
         w0, w1, w2, w3 = chain_w
-        FFN_PUMPS = [[], [], [b0], [(w0, 0)]]
-        MID_PUMPS = [[b1], [(w1, 0)]]
-        ATT_PUMPS = [[], [b2, b4], [(w0, 1)], [(w2, 0)], [], [b3]]
-        END_PUMPS = [(w1, 1), (w2, 1), (w3, 0), b5, (chain_q, 0), (chain_e, 0), (w3, 1), (chain_o, 0), (chain_q, 1),
-                     (chain_e, 1), (chain_o, 1), (chain_k, 0), (chain_v, 0), (chain_k, 1), (chain_v, 1)]
+        FFN_PUMPS = [[], [], [b0, (w0, 0)], [b1, (w1, 0)]]
+        MID_PUMPS = [[(w0, 1)], [(w2, 0)]]
+        ATT_PUMPS = [[], [b2], [], [(w1, 1), b4], [], []]
+        KV_PUMPS = [[], [b3], [(w3, 0), (w2, 1)]]
+        END_PUMPS = [(chain_o, 0), b5, (chain_e, 0), (chain_o, 1), (chain_q, 0), (chain_k, 0), (chain_va, 0),
+                     (chain_q, 1), (w3, 1), (chain_k, 1), (chain_va, 1), (chain_vb, 0), (chain_e, 1), (chain_vb, 1)]
 
     def swapped(buf, val, order, unit):
         if order == YLH:
@@ -364,19 +369,8 @@
             r.h2t[0] = nt(r.sa[...], r.h2[...]).astype(BF)
             c_h2t.start()
             c_dy.wait()
-        if k == 1:
-            c_h2t.wait()
-        if k > 0:
-            grad_wi(k - 1)
-        else:
-            r.ctt[0] = nt(r.sa[...], r.ctx[...]).astype(BF)
-            c_ctt.start()
-        c_at(k).wait()
-        wb = nn(r.at[k, 0 : 2 * Q, :], r.dyb[...]) + nn(r.atr[k], r.dyo[...])
-        r.wb[k, 0] = wb[0:Q, :].astype(BF)
-        r.wb[k, 1] = wb[Q : 2 * Q, :].astype(BF)
         if fused:
-            y_wb(k).start()
+            pump(FFN_PUMPS[k])
         rows = slice(k * FC, (k + 1) * FC)
         part_d = nt(r.duf[...], r.w_in[:, rows])
         part_o = nn(r.a[0:H, :], r.w_back[rows, :])
@@ -386,9 +380,20 @@
         else:
             r.oacc[...] += part_o
             r.dacc[...] += part_d
+        c_at(k).wait()
+        wb = nn(r.at[k, 0 : 2 * Q, :], r.dyb[...]) + nn(r.atr[k], r.dyo[...])
+        r.wb[k, 0] = wb[0:Q, :].astype(BF)
+        r.wb[k, 1] = wb[Q : 2 * Q, :].astype(BF)
         if fused:
-            pump(FFN_PUMPS[k])
-    grad_wi(NF - 1)
+            y_wb(k).start()
+        if k == 0:
+            c_h2t.wait()
+        grad_wi(k)
+        if k == 0:
+            r.ctt[0] = nt(r.sa[...], r.ctx[...]).astype(BF)
+            c_ctt.start()
+            r.h1t[0] = nt(r.sa[...], r.h1[...]).astype(BF)
+            c_h1t.start()
 
     if fused:
         pump(MID_PUMPS[0])
@@ -410,7 +415,9 @@
     c_dm = rc(sl.c_dm, r.dmb.at[1 - c], r.dmr, to_core)
     c_dm.start()
     r.dctx[...] = (nt(r.dmb[0], r.wo[:, 0:HC]) + nt(r.dmb[1], r.wo[:, HC : 2 * HC])).astype(BF)
-    r.o_layer[...] = (r.mid[0:H, :] + r.oacc[...]).astype(BF)
+    r.s_layer[...] = (r.mid[0:H, :] + r.oacc[...]).astype(BF)
+    outs = [pltpu.make_async_copy(r.s_layer, r.o_layer, r.osem.at[0]), pltpu.make_async_copy(r.s_x, r.o_x, r.osem.at[1])]
+    outs[0].start()
     if fused:
         pump(MID_PUMPS[1])
 
@@ -478,18 +485,26 @@
     r.dqkv[2, 1] = dv[:, HC : 2 * HC]
     c_g(2).start()
 
+    if fused:
+        pump(KV_PUMPS[0])
+
     def wgrad(i):
         c_g(i).wait()
         return nn(r.h1t[0], r.dqkv[i, c]) + nn(r.h1t[1], r.dqr[i])
 
     c_h1t.wait()
-    swap_rows(r.gq, slice(0, HC), wgrad(0), U)
+    r.gq[...] = wgrad(0).astype(BF)
     if fused:
         st_copy(chain_q, 0).start()
     r.gk[...] = wgrad(1).astype(BF)
     if fused:
         st_copy(chain_k, 0).start()
-    r.gv[:, 0:HC] = wgrad(2).astype(BF)
+        pump(KV_PUMPS[1])
+    gv = wgrad(2).astype(BF)
+    r.gva[...] = gv[:, 0:VW]
+    r.gvb[:, 0 : HC - VW] = gv[:, VW:HC]
+    if fused:
+        st_copy(chain_va, 0).start()
 
     acc = None
     for i, w in enumerate((r.wq, r.wk, r.wv)):
@@ -508,12 +523,15 @@
             dg = dn * ga
             m1 = jnp.sum(dg, axis=1, keepdims=True) * inv_d
             m2 = jnp.sum(dg * xh, axis=1, keepdims=True) * inv_d
-            r.o_x[rows, :] = r.dmid[rows, :] + r.rs1[rows, 0:1] * (dg - m1 - xh * m2)
+            r.s_x[rows, :] = r.dmid[rows, :] + r.rs1[rows, 0:1] * (dg - m1 - xh * m2)
+    outs[1].start()
     r.gvec[0:1, :] = gsum
+    if fused:
+        pump(KV_PUMPS[2])
     gains = jnp.concatenate([r.gvec[0:2, :], jnp.zeros((126, D), F32)], axis=0).astype(BF)
-    r.gv[:, HC:GN] = nt(r.sa[...], gains).astype(BF)
-    if fused:
-        st_copy(chain_v, 0).start()
+    r.gvb[:, HC - VW : VW] = nt(r.sa[...], gains).astype(BF)
+    if fused:
+        st_copy(chain_vb, 0).start()
 
     de = nt(r.dsk[...], r.k[0:H, :]) + nt(r.dsv[...], r.v[0:H, :])
     de = jnp.where(r.sel_t[:, 0:H] > 0.5, de, 0.0).astype(BF)
@@ -523,38 +541,69 @@
         r.ge[b * EB : (b + 1) * EB, :] = de[j * EB : (j + 1) * EB, :]
 
     if not fused:
+        for cp in outs:
+            cp.wait()
         return
 
     st_copy(chain_e, 0).start()
     pump(END_PUMPS)
 
     fin = r.fin
-    for k in range(NF):
-        fin[:, k * HC : (k + 1) * HC] = st_last(chain_w[k])
-    at = NF * HC
-    for chain in (chain_o, chain_q, chain_v, chain_k):
-        width = chain[1].shape[1]
-        fin[:, at : at + width] = st_last(chain)
-        at += width
     half = U // 2
-    c_fin = rc(sl.c_fin, fin.at[pl.ds(pl.multiple_of((1 - c) * half, 8), half)], r.finr, to_core)
-    c_fin.start()
+    mine = pl.ds(pl.multiple_of(c * half, 8), half)
+    first = (w0, w1, w2, w3, chain_o, chain_q, chain_k)
+    homes = [(r.s_in, k * FC) for k in range(NF)] + [(r.s_out, 0), (r.s_q, 0), (r.s_k, 0), (r.s_v, 0)]
+    n1 = len(first) * HC
+
+    def send_out(src, dst):
+        cp = pltpu.make_async_copy(src, dst, r.osem.at[len(outs)])
+        cp.start()
+        outs.append(cp)
+
+    def c_fin(i):
+        cols = pl.ds(0, n1) if i == 0 else pl.ds(n1, GN)
+        rows = pl.ds(pl.multiple_of((1 - c) * half, 8), half)
+        return rc(sl.c_fin + i, fin.at[rows, cols], r.finr.at[:, cols], to_core)
+
+    def put(i):
+        dst, base = homes[i]
+        at = i * HC
+        dst[:, pl.ds(pl.multiple_of(base + c * HC, 128), HC)] = fin[mine, at : at + HC]
+        dst[:, pl.ds(pl.multiple_of(base + (1 - c) * HC, 128), HC)] = r.finr[:, at : at + HC]
+
+    def take(i):
+        fin[:, i * HC : (i + 1) * HC] = st_last(first[i])
+
+    for i in (0, 1, 2):
+        take(i)
     hi_wb().wait()
-    r.o_back[...] = r.wb[2 * hi + lo, y].astype(F32) + r.wb3[...].astype(F32)
-    r.o_e[...] = st_last(chain_e)
-    c_fin.wait()
-    mine = pl.ds(pl.multiple_of(c * half, 8), half)
-
-    def put(dst, base, src_col):
-        dst[:, pl.ds(pl.multiple_of(base + c * HC, 128), HC)] = fin[mine, src_col : src_col + HC]
-        dst[:, pl.ds(pl.multiple_of(base + (1 - c) * HC, 128), HC)] = r.finr[:, src_col : src_col + HC]
-
-    for k in range(NF):
-        put(r.o_in, k * FC, k * HC)
-    for dst, at in ((r.o_out, NF * HC), (r.o_q, (NF + 1) * HC), (r.o_v, (NF + 2) * HC), (r.o_k, (NF + 2) * HC + GN)):
-        put(dst, 0, at)
-    at = (NF + 3) * HC
-    r.o_g[...] = fin[mine, at : at + 128] + r.finr[:, at : at + 128]
+    r.s_back[...] = r.wb[2 * hi + lo, y].astype(F32) + r.wb3[...].astype(F32)
+    send_out(r.s_back, r.o_back)
+    for i in (4, 5, 3, 6):
+        take(i)
+    c_fin(0).start()
+    fin[:, n1 : n1 + VW] = st_last(chain_va)
+    r.s_e[...] = st_last(chain_e)
+    send_out(r.s_e, r.o_e)
+    c_fin(0).wait()
+    for i in range(len(first)):
+        put(i)
+    for src, dst in ((r.s_in, r.o_in), (r.s_out, r.o_out), (r.s_q, r.o_q), (r.s_k, r.o_k)):
+        send_out(src, dst)
+    fin[:, n1 + VW : n1 + GN] = st_last(chain_vb)
+    c_fin(1).start()
+    c_fin(1).wait()
+    put(len(first))
+    at = n1 + HC
+    r.s_g[...] = fin[mine, at : at + 128] + r.finr[:, at : at + 128]
+    send_out(r.s_v, r.o_v)
+    send_out(r.s_g, r.o_g)
+    for cp in outs:
+        cp.wait()
+
+
+def staged(name):
+    return f"s{name[1:]}"
 
 
 def hand_over(r, names):
@@ -586,8 +635,8 @@
 
     inputs = dict(
         x_in=(tokens.reshape(H, D), False),
-        seg_in=(seg_ids.reshape(1, H), True),
-        slot_in=(slot_doc.reshape(1, J), True),
+        seg_in=(seg_ids.reshape(1, H), False),
+        slot_in=(slot_doc.reshape(1, J), False),
         e_in=(proj_e, False),
         ga=(g_attn, True),
         wq_in=(w_query, False),
@@ -607,7 +656,8 @@
         go=((D // 2, HC), BF),
         gq=((D // 2, HC), BF),
         gk=((D // 2, HC), BF),
-        gv=((D // 2, GN), BF),
+        gva=((D // 2, GN // 2), BF),
+        gvb=((D // 2, GN // 2), BF),
         ge=((J, H), BF),
     )
     outs = dict(o_layer=((H, D), BF), o_x=((H, D), F32))
@@ -625,7 +675,7 @@
     else:
         outs.update(parts)
     scratch = dict(
-        xb=((T, D), BF), eb=((T, J), BF), segf=((2, 8, H), F32),
+        xb=((T, D), BF), eb=((T, J), BF), segs=((2, 1, H), jnp.int32), slot=((1, J), jnp.int32),
         wq=((D, D), BF), wk=((D, D), BF), wv=((D, D), BF), wo=((D, D), BF),
         w_in=((D, FF), BF), w_back=((FF, D), BF),
         dyb=((T, D), BF), dyo=((T, D), BF),
@@ -655,32 +705,35 @@
             go1=((4 * U, HC), BF), go2=((2 * U, HC), BF), go3=((U, HC), BF),
             gq1=((4 * U, HC), BF), gq2=((2 * U, HC), BF), gq3=((U, HC), BF),
             gk1=((4 * U, HC), BF), gk2=((2 * U, HC), BF), gk3=((U, HC), BF),
-            gv1=((4 * U, GN), BF), gv2=((2 * U, GN), BF), gv3=((U, GN), BF),
+            gva1=((4 * U, GN // 2), BF), gva2=((2 * U, GN // 2), BF), gva3=((U, GN // 2), BF),
+            gvb1=((4 * U, GN // 2), BF), gvb2=((2 * U, GN // 2), BF), gvb3=((U, GN // 2), BF),
             ge1=((4 * EB, H), BF), ge2=((2 * EB, H), BF), ge3=((EB, H), BF),
             fin=((U, NF * HC + 3 * HC + GN), F32), finr=((U // 2, NF * HC + 3 * HC + GN), F32),
         )
     counts = dict(
         x_seg=1, x_e=1, x_x=1, x_dy=1, c_pk=1, c_pv=1, c_h1t=1, c_h2t=1, c_dy=1, c_ctt=1, c_at=NF, c_du=NF, c_dm=1,
-        c_ds=D // 128, c_g=3, y_wb=NF, wi=3 * NF, lo_wb=2, hi_wb=1, go=3, gq=3, gk=3, gv=3, ge=3, c_fin=1,
+        c_ds=D // 128, c_g=3, y_wb=NF, wi=3 * NF, lo_wb=2, hi_wb=1, go=3, gq=3, gk=3, gva=3, gvb=3, ge=3, c_fin=2,
     )
     sl, count = SimpleNamespace(), 0
     for name, n in counts.items():
         setattr(sl, name, count)
         count += n
+    scratch.update((staged(n), v) for n, v in outs.items() if n[0] == "o")
     names = [*inputs, *outs, *scratch]
 
     def body(*refs):
         r = SimpleNamespace(**dict(zip(names, refs)))
-        r.lsem, r.ssem, r.rsem = refs[len(names) :]
+        r.osem, r.lsem, r.ssem, r.rsem = refs[len(names) :]
         layer_body(fused, r, sl)
 
     res = pl.pallas_call(
         body,
         out_shape=[jax.ShapeDtypeStruct(sh, dt) for sh, dt in outs.values()],
         in_specs=[pl.BlockSpec(memory_space=pltpu.VMEM if v else pl.ANY) for _, v in inputs.values()],
-        out_specs=[pl.BlockSpec(memory_space=pltpu.VMEM) for _ in outs],
+        out_specs=[pl.BlockSpec(memory_space=pl.ANY if n[0] == "o" else pltpu.VMEM) for n in outs],
         scratch_shapes=[pltpu.VMEM(sh, dt) for sh, dt in scratch.values()]
-        + [pltpu.SemaphoreType.DMA((12,)), pltpu.SemaphoreType.DMA((count,)), pltpu.SemaphoreType.DMA((count,))],
+        + [pltpu.SemaphoreType.DMA((10,))]
+        + [pltpu.SemaphoreType.DMA((14,)), pltpu.SemaphoreType.DMA((count,)), pltpu.SemaphoreType.DMA((count,))],
         compiler_params=pltpu.CompilerParams(
             collective_id=0, has_side_effects=True, vmem_limit_bytes=60 * 1024 * 1024
         ),
@@ -737,8 +790,9 @@
 
     wi = jnp.stack([whole(o.wi[f], True) for f in range(NF)], axis=1).reshape(D, FF)
     wo = whole(o.go, True)
-    wqkv = [whole(o.gq, False), whole(o.gk, True), whole(o.gv[:, :HC], True)]
-    gains = rows_back(o.gv[:, HC:], True)
+    gv = jnp.concatenate([o.gva, o.gvb], axis=1)
+    wqkv = [whole(o.gq, True), whole(o.gk, True), whole(gv[:, :HC], True)]
+    gains = rows_back(gv[:, HC:], True)
     gfull = lax.dynamic_update_slice(jnp.zeros((8, 2, U, 128), F32), gains[:, None], (0, x, 0, 0)).reshape(D, 128)
     wb = o.wb.astype(F32).reshape(NF * 2, 1, Q, D)
     wb = lax.dynamic_update_slice(jnp.zeros((NF * 2, 4, Q, D), F32), wb, (0, s, 0, 0)).reshape(FF, D)

time: 81.3 us -> 75.9 us (0.934)
  Pallas kernels: 80.2 us -> 74.8 us
    pallas_call x1, Pallas kernels: 77 us -> 71.5 us  [run_layer(): pl.pallas_call(body, out_shape=[jax.ShapeDtypeStruct(sh, dt) for sh, dt i...]
where the time goes in v3:
time: 75.9 us; the launch traced here: 75.6 us
  Pallas kernels  74.8 us (99%)
  between operations  0.82 us (1%)
    pallas_call x1, Pallas kernels, run_layer(): pl.pallas_call(body, out_shape=[jax.ShapeDtypeStruct(sh, dt) for sh, dt i...  71.5 us
    pallas_call x1, Pallas kernels, run_layer(): pl.pallas_call(tail, out_shape=[jax.ShapeDtypeStruct(sh, dt) for sh, dt i...  3.27 us

profile of v3, /device:TPU:0, one launch (start us, length us, event | category | flops | bytes accessed | tf_op | source)
XLA Modules:
  0.0 75.6 jit_solution(13487623577628098154)
XLA Ops:
  0.6 71.5 %shard_map.230 = (bf16[128,768]{1,0:T(8,128)(2,1)}, f32[128,768]{1,0:T(8,128)}, f32[24,128]{1,0:T(8,128)}, f32[24,768]{1,0:T(8,128)}, f32[24,768]{1,0:T(8,128)},...) custom-call(bf16[128,768]{1,0:T(8,128)(2,1)} %bitcast.3, ...), custom_call_target="tpu_custom_call" | custom-call | flops 12000000000 | bytes 24000000 | tf_op jit(solution)/shard_map/pallas_call | solution.py:729
  72.2 3.3 %shard_map.231 = (bf16[1,128,768]{2,1,0:T(8,128)(2,1)}, f32[1,128,768]{2,1,0:T(8,128)}, f32[24,768]{1,0:T(8,128)}, f32[24,768]{1,0:T(8,128)}, f32[24,768]{1,0:T(...) custom-call(bf16[128,768]{1,0:T(8,128)(2,1)} %get-tuple-element.32.r, ...), custom_call_target="tpu_custom_call" | custom-call | tf_op jit(solution)/shard_map/pallas_call | solution.py:760

commit v4 on v3

--- a/solution.py
+++ b/solution.py
@@ -40,12 +40,11 @@
             for o in range(unit):
                 sel_a[x, b * unit + o, (2 * j + x) * unit + o] = 1
     q = ff // 32
-    sel_c = np.zeros((2, 2, 2 * q, ff // 4), np.float32)
+    sel_c = np.zeros((2, 4 * q, ff // 4), np.float32)
     for x in range(2):
-        for c in range(2):
-            for y in range(2):
-                for o in range(q):
-                    sel_c[x, c, y * q + o, (y * 4 + x * 2 + c) * q + o] = 1
+        for b in range(4):
+            for o in range(q):
+                sel_c[x, b * q + o, (b // 2 * 4 + x * 2 + b % 2) * q + o] = 1
     return sel_a, sel_c
 
 
@@ -67,7 +66,7 @@
     NF = r.w_in.shape[1] // FC
     HC = D // 2
     U = D // 16
-    Q = r.wb.shape[2]
+    Q = r.wb.shape[1] // 4
     scale = HEAD_DIM ** (-0.5)
 
     loads = []
@@ -97,8 +96,7 @@
     l_dy = load(r.dy_in, r.dyb.at[pl.ds(0, H)])
     l_sa = load(r.sa_in.at[x], r.sa)
     l_wo = load(r.wo_in, r.wo)
-    l_sc0 = load(r.sc_in.at[x, c], r.sc.at[pl.ds(0, 2 * Q)])
-    l_sc1 = load(r.sc_in.at[x, 1 - c], r.sc.at[pl.ds(2 * Q, 2 * Q)])
+    l_sc = load(r.sc_in.at[x], r.sc)
     l_w_in = load(r.w_in_in, r.w_in)
     l_w_back = load(r.w_back_in, r.w_back)
 
@@ -109,6 +107,11 @@
     x_x = rc(sl.x_x, r.x_in, r.xb.at[pl.ds(H, H)], to_x)
     x_dy = rc(sl.x_dy, r.dy_in, r.dyb.at[pl.ds(H, H)], to_x)
     x_x.start()
+    if fused:
+        own_rows, far_rows = pl.ds(0, H), pl.ds(H, H)
+        l_dyf = rc(sl.l_dy, r.dy_in, r.dyf.at[own_rows], to_lo)
+        x_dyf = rc(sl.x_dyf, r.dyf.at[own_rows], r.dyf.at[far_rows], to_x)
+        l_dyf.start()
 
     rows_i = lax.broadcasted_iota(jnp.int32, (T, T), 0)
     cols_i = lax.broadcasted_iota(jnp.int32, (T, T), 1)
@@ -209,28 +212,42 @@
         raw = nxt
     fwd_ctx(NP - 1)
 
+    if fused:
+        l_dyf.wait()
+        x_dyf.start()
+
+    def l_h2(p):
+        rows = pl.ds(p * NR, NR)
+        return rc(sl.l_h2 + p, r.h2.at[rows], r.h2f.at[rows], to_lo)
+
+    def x_h2(p):
+        return rc(sl.x_h2 + p, r.h2f.at[pl.ds(p * NR, NR)], r.h2f.at[pl.ds(H + p * NR, NR)], to_x)
+
     l_wo.wait()
-    r.mid[...] = r.xb[...].astype(F32) + nn(r.ctx[...], r.wo[...])
-    norm_into(r.mid, gf, r.xh2, r.rs2, r.h2, 0, T)
+    for rows in (own, far):
+        r.mid[rows, :] = r.xb[rows, :].astype(F32) + nn(r.ctx[rows, :], r.wo[...])
+    norm_into(r.mid, gf, r.xh2, r.rs2, r.h2, 0, H)
+    if fused:
+        for p in range(H // NR):
+            l_h2(p).start()
+    norm_into(r.mid, gf, r.xh2, r.rs2, r.h2, H, H)
     x_dy.wait()
     l_dy.wait()
-    c_dy = rc(sl.c_dy, r.dyb, r.dyo, to_core)
-    c_dy.start()
+    c_dy = rc(sl.c_dy, r.dyh.at[1 - c], r.dyr, to_core)
     l_w_in.wait()
     l_w_back.wait()
-    l_sc0.wait()
-    l_sc1.wait()
+    l_sc.wait()
     c_h2t = rc(sl.c_h2t, r.h2t.at[0], r.h2t.at[1], to_core)
     c_ctt = rc(sl.c_ctt, r.ctt.at[0], r.ctt.at[1], to_core)
 
-    def c_at(f):
-        return rc(sl.c_at + f, r.at.at[f, pl.ds(2 * Q, 2 * Q)], r.atr.at[f], to_core)
+    def c_at(k):
+        return rc(sl.c_at + k, r.at.at[k], r.atr.at[k], to_core)
 
     def c_du(f):
         return rc(sl.c_du + f, r.du.at[f, 1 - c], r.dur.at[f], to_core)
 
     def y_wb(k):
-        return rc(sl.y_wb + k, r.wb.at[k, 1 - y], r.wb1.at[k], to_y)
+        return rc(sl.y_wb + k, r.wb.at[k, rows16((1 - y) * 2 * Q, 2 * Q)], r.wb1.at[k], to_y)
 
     bits = dict(y=(y, to_y), l=(lo, to_lo), h=(hi, to_hi))
 
@@ -246,46 +263,39 @@
     def rows16(start, n):
         return pl.ds(pl.multiple_of(start, 16), n)
 
-    GN = HC + 128
-    VW = GN // 2
+    GN = 128
+    VW = 256
     EB = J // 8
     if fused:
         chain_w = [
-            (LYH, r.wi.at[k], (r.wi1.at[k], r.wi2.at[k], r.wi3.at[k]), sl.wi + 3 * k, U)
+            (LYH if k % 2 else YLH, r.wi.at[k], (r.wi1.at[k], r.wi2.at[k], r.wi3.at[k]), sl.wi + 3 * k, U)
             for k in range(NF)
         ]
-        chain_o = (YLH, r.go, (r.go1, r.go2, r.go3), sl.go, U)
-        chain_q = (YLH, r.gq, (r.gq1, r.gq2, r.gq3), sl.gq, U)
+        chain_o = (LYH, r.go, (r.go1, r.go2, r.go3), sl.go, U)
+        chain_q = (LYH, r.gq, (r.gq1, r.gq2, r.gq3), sl.gq, U)
         chain_k = (YLH, r.gk, (r.gk1, r.gk2, r.gk3), sl.gk, U)
         chain_va = (YLH, r.gva, (r.gva1, r.gva2, r.gva3), sl.gva, U)
         chain_vb = (YLH, r.gvb, (r.gvb1, r.gvb2, r.gvb3), sl.gvb, U)
+        chain_g = (YLH, r.gg, (r.gg1, r.gg2, r.gg3), sl.gg, U)
         chain_e = (LYH, r.ge, (r.ge1, r.ge2, r.ge3), sl.ge, EB)
 
     def add_into(dst, idx, src):
         dst[idx] = (dst[idx].astype(F32) + src.astype(F32)).astype(BF)
 
-    def lo_wb(p):
-        return rc(sl.lo_wb + p, r.wb.at[2 * p + 1 - lo, y], r.wb2.at[p], to_lo)
-
     def hi_wb():
-        return rc(sl.hi_wb, r.wb.at[2 * (1 - hi) + lo, y], r.wb3, to_hi)
+        return rc(sl.hi_wb, r.wb.at[1 - hi, rows16(y * 2 * Q, 2 * Q)], r.wb2, to_hi)
 
     def pump_wb(k):
-        if k < 4:
+        if k < 2:
             y_wb(k).wait()
-            add_into(r.wb, (k, y), r.wb1[k])
-
-            @pl.when(lo == 1 - k % 2)
-            def _():
-                lo_wb(k // 2).start()
-        else:
-            p = k - 4
-            lo_wb(p).wait()
-            add_into(r.wb, (2 * p + lo, y), r.wb2[p])
-
-            @pl.when(hi == 1 - p)
+            add_into(r.wb, (k, rows16(y * 2 * Q, 2 * Q), slice(None)), r.wb1[k])
+
+            @pl.when(hi == 1 - k)
             def _():
                 hi_wb().start()
+        else:
+            l_h2(k - 2).wait()
+            x_h2(k - 2).start()
 
     def pump(steps):
         for step in steps:
@@ -322,14 +332,15 @@
     GR = 32
 
     if fused:
-        b0, b1, b2, b3, b4, b5 = [(None, k) for k in range(6)]
+        b0, b1, h0, h1 = [(None, k) for k in range(4)]
         w0, w1, w2, w3 = chain_w
-        FFN_PUMPS = [[], [], [b0, (w0, 0)], [b1, (w1, 0)]]
-        MID_PUMPS = [[(w0, 1)], [(w2, 0)]]
-        ATT_PUMPS = [[], [b2], [], [(w1, 1), b4], [], []]
-        KV_PUMPS = [[], [b3], [(w3, 0), (w2, 1)]]
-        END_PUMPS = [(chain_o, 0), b5, (chain_e, 0), (chain_o, 1), (chain_q, 0), (chain_k, 0), (chain_va, 0),
-                     (chain_q, 1), (w3, 1), (chain_k, 1), (chain_va, 1), (chain_vb, 0), (chain_e, 1), (chain_vb, 1)]
+        FFN_PUMPS = [[], [], [h0], [h1]]
+        MID_PUMPS = [[(w0, 0)], [(w1, 0)]]
+        ATT_PUMPS = [[(w2, 0)], [(w0, 1), (w3, 0)], [], [], [(w1, 1)], []]
+        KV_PUMPS = [[(chain_o, 0)], [], [(w2, 1), b0]]
+        END_PUMPS = [(w3, 1), b1, (chain_q, 0), (chain_e, 0), (chain_o, 1), (chain_k, 0), (chain_va, 0), (chain_vb, 0),
+                     (chain_g, 0), (chain_k, 1), (chain_va, 1), (chain_q, 1), (chain_vb, 1), (chain_e, 1),
+                     (chain_g, 1)]
 
     def swapped(buf, val, order, unit):
         if order == YLH:
@@ -337,64 +348,119 @@
         else:
             swap_rows(buf, slice(0, val.shape[1]), val, unit)
 
-    def grad_wi(k):
-        c_du(k).wait()
-        val = nn(r.h2t[0], r.du[k, c]) + nn(r.h2t[1], r.dur[k])
-        if not fused:
-            r.wi[k] = val.astype(BF)
-            return
-        swapped(chain_w[k][1], val, chain_w[k][0], U)
-        st_copy(chain_w[k], 0).start()
-
-    for k in range(NF):
-        for b in range(FC // SB):
-            off = k * FC + b * SB
-            u = nn(r.h2[...], r.w_in[:, off : off + SB])
-            g = nt(r.dyb[...], r.w_back[off : off + SB, :])
-            for m in range(T // GR):
-                rr = slice(m * GR, (m + 1) * GR)
-                um = u[rr, :]
-                u2 = um * um
-                th = jnp.tanh(um * (GELU_C + (GELU_C * GELU_K) * u2))
-                half = 0.5 + 0.5 * th
-                r.a[rr, b * SB : (b + 1) * SB] = (um * half).astype(BF)
-                slope = half + (um * half) * ((1.0 - th) * (GELU_C + (3.0 * GELU_C * GELU_K) * u2))
-                r.duf[rr, b * SB : (b + 1) * SB] = (slope * g[rr, :]).astype(BF)
-        r.at[k] = nt(r.sc[...], r.a[...]).astype(BF)
-        c_at(k).start()
-        r.du[k, 0] = r.duf[:, 0:HC]
-        r.du[k, 1] = r.duf[:, HC : 2 * HC]
-        c_du(k).start()
-        if k == 0:
-            r.h2t[0] = nt(r.sa[...], r.h2[...]).astype(BF)
-            c_h2t.start()
-            c_dy.wait()
+    def dense(k):
+        wi = nn(r.h2t[0], r.du[k, c]) + nn(r.h2t[1], r.dur[k])
         if fused:
-            pump(FFN_PUMPS[k])
+            swapped(chain_w[k][1], wi, chain_w[k][0], U)
+        else:
+            r.wi[k] = wi.astype(BF)
+
+    def send_dense(k):
+        if fused:
+            st_copy(chain_w[k], 0).start()
+
+    NW = r.wb.shape[0]
+
+    def act_rows():
+        for h in range(2):
+            r.dyh[h, 0:T, :] = r.dyb[:, h * HC : (h + 1) * HC]
+        if fused:
+            x_dyf.wait()
+            for h in range(2):
+                r.dyh[h, T : 2 * T, :] = r.dyf[:, h * HC : (h + 1) * HC]
+        c_dy.start()
+        if fused:
+            for p in range(H // NR):
+                x_h2(p).wait()
+            for k in range(NW):
+                for b in range(NB):
+                    cols = slice(b * SB, (b + 1) * SB)
+                    u = nn(r.h2f[...], r.w_in[:, pl.ds(pl.multiple_of((lo + 2 * k) * FC + b * SB, SB), SB)])
+                    for m in range(T // GR):
+                        rr = slice(m * GR, (m + 1) * GR)
+                        um = u[rr, :]
+                        th = jnp.tanh(um * (GELU_C + (GELU_C * GELU_K) * (um * um)))
+                        r.af[k, rr, cols] = (um * (0.5 + 0.5 * th)).astype(BF)
+        for k in range(NW):
+            r.at[k, :, 0:T] = nt(r.sc[...], r.a[lo + 2 * k if fused else k]).astype(BF)
+            if fused:
+                r.at[k, :, T : 2 * T] = nt(r.sc[...], r.af[k]).astype(BF)
+            c_at(k).start()
+
+    def grad_wb():
+        c_dy.wait()
+        for k in range(NW):
+            c_at(k).wait()
+        for k in range(NW):
+            r.wb[k] = (nn(r.at[k], r.dyh[c]) + nn(r.atr[k], r.dyr[...])).astype(BF)
+        if fused:
+            for k in range(NW):
+                y_wb(k).start()
+
+    def back(k):
         rows = slice(k * FC, (k + 1) * FC)
-        part_d = nt(r.duf[...], r.w_in[:, rows])
-        part_o = nn(r.a[0:H, :], r.w_back[rows, :])
+        part_d = nt(r.duf[k % 2], r.w_in[:, rows])
+        part_o = nn(r.a[k, 0:H, :], r.w_back[rows, :])
         if k == 0:
             r.oacc[...] = part_o
             r.dacc[...] = part_d
         else:
             r.oacc[...] += part_o
             r.dacc[...] += part_d
-        c_at(k).wait()
-        wb = nn(r.at[k, 0 : 2 * Q, :], r.dyb[...]) + nn(r.atr[k], r.dyo[...])
-        r.wb[k, 0] = wb[0:Q, :].astype(BF)
-        r.wb[k, 1] = wb[Q : 2 * Q, :].astype(BF)
-        if fused:
-            y_wb(k).start()
-        if k == 0:
-            c_h2t.wait()
-        grad_wi(k)
-        if k == 0:
-            r.ctt[0] = nt(r.sa[...], r.ctx[...]).astype(BF)
-            c_ctt.start()
-            r.h1t[0] = nt(r.sa[...], r.h1[...]).astype(BF)
-            c_h1t.start()
-
+
+    NB = FC // SB
+
+    def hidden(k, b):
+        off = k * FC + b * SB
+        cols = slice(b * SB, (b + 1) * SB)
+        r.u[k % 2, :, cols] = nn(r.h2[...], r.w_in[:, off : off + SB])
+        r.g[k % 2, :, cols] = nt(r.dyb[...], r.w_back[off : off + SB, :])
+
+    def gelu(k, b):
+        cols = slice(b * SB, (b + 1) * SB)
+        for m in range(T // GR):
+            rr = slice(m * GR, (m + 1) * GR)
+            um = r.u[k % 2, rr, cols]
+            u2 = um * um
+            th = jnp.tanh(um * (GELU_C + (GELU_C * GELU_K) * u2))
+            half = 0.5 + 0.5 * th
+            act = um * half
+            r.a[k, rr, cols] = act.astype(BF)
+            slope = half + act * ((1.0 - th) * (GELU_C + (3.0 * GELU_C * GELU_K) * u2))
+            r.duf[k % 2, rr, cols] = (slope * r.g[k % 2, rr, cols]).astype(BF)
+
+    for b in range(NB):
+        hidden(0, b)
+    for k in range(NF):
+        for b in range(NB):
+            if k + 1 < NF:
+                hidden(k + 1, b)
+            gelu(k, b)
+        if k > 0:
+            back(k - 1)
+            if fused:
+                pump(FFN_PUMPS[k])
+            if k == 1:
+                c_h2t.wait()
+            c_du(k - 1).wait()
+            dense(k - 1)
+        else:
+            r.h2t[0] = nt(r.sa[...], r.h2[...]).astype(BF)
+        r.du[k, 0] = r.duf[k % 2, :, 0:HC]
+        r.du[k, 1] = r.duf[k % 2, :, HC : 2 * HC]
+        c_du(k).start()
+        if k > 0:
+            send_dense(k - 1)
+        else:
+            c_h2t.start()
+    back(NF - 1)
+    r.ctt[0] = nt(r.sa[...], r.ctx[...]).astype(BF)
+    r.h1t[0] = nt(r.sa[...], r.h1[...]).astype(BF)
+    c_ctt.start()
+    c_h1t.start()
+
+    c_du(NF - 1).wait()
+    dense(NF - 1)
     if fused:
         pump(MID_PUMPS[0])
     gsum = None
@@ -414,6 +480,7 @@
     r.gvec[1:2, :] = gsum
     c_dm = rc(sl.c_dm, r.dmb.at[1 - c], r.dmr, to_core)
     c_dm.start()
+    send_dense(NF - 1)
     r.dctx[...] = (nt(r.dmb[0], r.wo[:, 0:HC]) + nt(r.dmb[1], r.wo[:, HC : 2 * HC])).astype(BF)
     r.s_layer[...] = (r.mid[0:H, :] + r.oacc[...]).astype(BF)
     outs = [pltpu.make_async_copy(r.s_layer, r.o_layer, r.osem.at[0]), pltpu.make_async_copy(r.s_x, r.o_x, r.osem.at[1])]
@@ -421,8 +488,11 @@
     if fused:
         pump(MID_PUMPS[1])
 
-    def c_ds(i):
-        return rc(sl.c_ds + i, r.pd.at[i], r.pdr.at[i], to_core)
+    act_rows()
+
+    def c_ds(g):
+        pair = pl.ds(2 * g, 2)
+        return rc(sl.c_ds + g, r.pd.at[pair], r.pdr.at[pair], to_core)
 
     def bwd_dp(i):
         cols = slice(i * 128, (i + 1) * 128)
@@ -445,9 +515,10 @@
         dsk = nn(draw[0:J], q2 * head_mask[0]) + nn(draw[J : 2 * J], q2 * head_mask[1])
         r.pd[i, 0] = dsk.astype(BF)
         r.pd[i, 1] = dsv.astype(BF)
-        c_ds(i).start()
         stack = jnp.concatenate([sk2 * head_mask[0], sk2 * head_mask[1]], axis=0)
         r.dqkv[0, i // 3, :, (i % 3) * 128 : (i % 3 + 1) * 128] = tn(draw, stack).astype(BF)
+        if i % 2:
+            c_ds(i // 2).start()
 
     dpf = bwd_dp(0)
     for i in range(NP):
@@ -459,9 +530,11 @@
         if i == 0:
             c_ctt.wait()
             c_dm.wait()
-            r.go[...] = (nn(r.ctt[0], r.dmb[c]) + nn(r.ctt[1], r.dmr[...])).astype(BF)
+            swapped(r.go, nn(r.ctt[0], r.dmb[c]) + nn(r.ctt[1], r.dmr[...]), LYH if fused else YLH, U)
             if fused:
                 st_copy(chain_o, 0).start()
+        if i == 1:
+            grad_wb()
         if fused:
             pump(ATT_PUMPS[i])
     bwd_out(NP - 1)
@@ -472,42 +545,52 @@
     c_g(0).start()
     for i in range(D // 128):
         cols = slice(i * 128, (i + 1) * 128)
-        c_ds(i).wait()
+        if i % 2 == 0:
+            c_ds(i // 2).wait()
         r.dsk[:, cols] = (r.pd[i, 0].astype(F32) + r.pdr[i, 0].astype(F32)).astype(BF)
         r.dsv[:, cols] = (r.pd[i, 1].astype(F32) + r.pdr[i, 1].astype(F32)).astype(BF)
 
     dk = nn(r.me[...], r.dsk[...]).astype(BF)
+    dv = nn(r.me[...], r.dsv[...]).astype(BF)
     r.dqkv[1, 0] = dk[:, 0:HC]
     r.dqkv[1, 1] = dk[:, HC : 2 * HC]
-    c_g(1).start()
-    dv = nn(r.me[...], r.dsv[...]).astype(BF)
     r.dqkv[2, 0] = dv[:, 0:HC]
     r.dqkv[2, 1] = dv[:, HC : 2 * HC]
+    c_g(1).start()
     c_g(2).start()
 
-    if fused:
+    def wgrad(i):
+        return (nn(r.h1t[0], r.dqkv[i, c]) + nn(r.h1t[1], r.dqr[i])).astype(BF)
+
+    c_h1t.wait()
+    c_g(0).wait()
+    swapped(r.gq, wgrad(0), LYH if fused else YLH, U)
+    if fused:
+        st_copy(chain_q, 0).start()
         pump(KV_PUMPS[0])
-
-    def wgrad(i):
-        c_g(i).wait()
-        return nn(r.h1t[0], r.dqkv[i, c]) + nn(r.h1t[1], r.dqr[i])
-
-    c_h1t.wait()
-    r.gq[...] = wgrad(0).astype(BF)
-    if fused:
-        st_copy(chain_q, 0).start()
-    r.gk[...] = wgrad(1).astype(BF)
-    if fused:
-        st_copy(chain_k, 0).start()
-        pump(KV_PUMPS[1])
-    gv = wgrad(2).astype(BF)
-    r.gva[...] = gv[:, 0:VW]
-    r.gvb[:, 0 : HC - VW] = gv[:, VW:HC]
-    if fused:
-        st_copy(chain_va, 0).start()
-
+    de = nt(r.dsk[...], r.k[0:H, :]) + nt(r.dsv[...], r.v[0:H, :])
+    de = jnp.where(r.sel_t[:, 0:H] > 0.5, de, 0.0).astype(BF)
+    for b in range(8):
+        b2, b1, b0 = b // 4, (b // 2) % 2, b % 2
+        j = 4 * b0 + 2 * b2 + b1
+        r.ge[b * EB : (b + 1) * EB, :] = de[j * EB : (j + 1) * EB, :]
     acc = None
     for i, w in enumerate((r.wq, r.wk, r.wv)):
+        if i == 1:
+            r.dacc[...] = acc
+            c_g(1).wait()
+            c_g(2).wait()
+            r.gk[...] = wgrad(1)
+            gv = wgrad(2)
+            r.gva[...] = gv[:, 0:VW]
+            r.gvb[...] = gv[:, VW:HC]
+            if fused:
+                st_copy(chain_k, 0).start()
+                st_copy(chain_va, 0).start()
+                st_copy(chain_vb, 0).start()
+                st_copy(chain_e, 0).start()
+                pump(KV_PUMPS[1])
+            acc = r.dacc[...]
         for hf in range(2):
             part = nt(r.dqkv[i, hf], w[:, hf * HC : (hf + 1) * HC])
             acc = part if acc is None else acc + part
@@ -529,23 +612,15 @@
     if fused:
         pump(KV_PUMPS[2])
     gains = jnp.concatenate([r.gvec[0:2, :], jnp.zeros((126, D), F32)], axis=0).astype(BF)
-    r.gvb[:, HC - VW : VW] = nt(r.sa[...], gains).astype(BF)
-    if fused:
-        st_copy(chain_vb, 0).start()
-
-    de = nt(r.dsk[...], r.k[0:H, :]) + nt(r.dsv[...], r.v[0:H, :])
-    de = jnp.where(r.sel_t[:, 0:H] > 0.5, de, 0.0).astype(BF)
-    for b in range(8):
-        b2, b1, b0 = b // 4, (b // 2) % 2, b % 2
-        j = 4 * b0 + 2 * b2 + b1
-        r.ge[b * EB : (b + 1) * EB, :] = de[j * EB : (j + 1) * EB, :]
+    r.gg[...] = nt(r.sa[...], gains).astype(BF)
+    if fused:
+        st_copy(chain_g, 0).start()
 
     if not fused:
         for cp in outs:
             cp.wait()
         return
 
-    st_copy(chain_e, 0).start()
     pump(END_PUMPS)
 
     fin = r.fin
@@ -561,7 +636,7 @@
         outs.append(cp)
 
     def c_fin(i):
-        cols = pl.ds(0, n1) if i == 0 else pl.ds(n1, GN)
+        cols = pl.ds(0, n1) if i == 0 else pl.ds(n1, HC + GN)
         rows = pl.ds(pl.multiple_of((1 - c) * half, 8), half)
         return rc(sl.c_fin + i, fin.at[rows, cols], r.finr.at[:, cols], to_core)
 
@@ -574,24 +649,31 @@
     def take(i):
         fin[:, i * HC : (i + 1) * HC] = st_last(first[i])
 
-    for i in (0, 1, 2):
+    for i in (0, 1, 2, 3):
         take(i)
     hi_wb().wait()
-    r.s_back[...] = r.wb[2 * hi + lo, y].astype(F32) + r.wb3[...].astype(F32)
-    send_out(r.s_back, r.o_back)
-    for i in (4, 5, 3, 6):
+    r.finb[...] = r.wb[hi, rows16(y * 2 * Q, 2 * Q), :].astype(F32) + r.wb2[...].astype(F32)
+    c_finb = rc(sl.c_finb, r.finb.at[pl.ds(pl.multiple_of((1 - c) * Q, 8), Q)], r.finbr, to_core)
+    c_finb.start()
+    for i in (4, 6):
         take(i)
+    fin[:, n1 : n1 + VW] = st_last(chain_va)
+    take(5)
     c_fin(0).start()
-    fin[:, n1 : n1 + VW] = st_last(chain_va)
+    fin[:, n1 + VW : n1 + HC] = st_last(chain_vb)
     r.s_e[...] = st_last(chain_e)
     send_out(r.s_e, r.o_e)
+    fin[:, n1 + HC : n1 + HC + GN] = st_last(chain_g)
+    c_fin(1).start()
+    c_finb.wait()
+    r.s_back[:, pl.ds(pl.multiple_of(c * HC, 128), HC)] = r.finb[pl.ds(pl.multiple_of(c * Q, 8), Q), :]
+    r.s_back[:, pl.ds(pl.multiple_of((1 - c) * HC, 128), HC)] = r.finbr[...]
+    send_out(r.s_back, r.o_back)
     c_fin(0).wait()
     for i in range(len(first)):
         put(i)
     for src, dst in ((r.s_in, r.o_in), (r.s_out, r.o_out), (r.s_q, r.o_q), (r.s_k, r.o_k)):
         send_out(src, dst)
-    fin[:, n1 + VW : n1 + GN] = st_last(chain_vb)
-    c_fin(1).start()
     c_fin(1).wait()
     put(len(first))
     at = n1 + HC
@@ -630,7 +712,8 @@
     T = 2 * H
     HC, U, NF, Q = D // 2, D // 16, FF // D, FF // 32
     EB = J // 8
-    GN = HC + 128
+    NW, TW = (2, 2 * T) if fused else (NF, T)
+    GN, VW = 128, 256
     sel_a, sel_c = (jnp.asarray(m, BF) for m in selections(D, FF))
 
     inputs = dict(
@@ -651,13 +734,14 @@
         sc_in=(sel_c, False),
     )
     parts = dict(
-        wb=((NF, 2, Q, D), BF),
+        wb=((NW, 4 * Q, HC), BF),
         wi=((NF, D // 2, HC), BF),
         go=((D // 2, HC), BF),
         gq=((D // 2, HC), BF),
         gk=((D // 2, HC), BF),
-        gva=((D // 2, GN // 2), BF),
-        gvb=((D // 2, GN // 2), BF),
+        gva=((D // 2, VW), BF),
+        gvb=((D // 2, HC - VW), BF),
+        gg=((D // 2, GN), BF),
         ge=((J, H), BF),
     )
     outs = dict(o_layer=((H, D), BF), o_x=((H, D), F32))
@@ -678,7 +762,7 @@
         xb=((T, D), BF), eb=((T, J), BF), segs=((2, 1, H), jnp.int32), slot=((1, J), jnp.int32),
         wq=((D, D), BF), wk=((D, D), BF), wv=((D, D), BF), wo=((D, D), BF),
         w_in=((D, FF), BF), w_back=((FF, D), BF),
-        dyb=((T, D), BF), dyo=((T, D), BF),
+        dyb=((T, D), BF), dyh=((2, TW, HC), BF), dyr=((TW, HC), BF),
         sa=((D // 2, D), BF), sc=((4 * Q, FF // 4), BF),
         eye=((T, T), BF),
         h1=((T, D), BF), xh1=((T, D), F32), rs1=((T, 128), F32),
@@ -689,8 +773,8 @@
         pt=((D // 128, 2 * J, T), BF), ctx=((T, D), BF),
         mid=((T, D), F32), xh2=((T, D), F32), rs2=((T, 128), F32), h2=((T, D), BF),
         h1t=((2, D // 2, T), BF), h2t=((2, D // 2, T), BF), ctt=((2, D // 2, T), BF),
-        a=((T, D), BF), duf=((T, D), BF), du=((NF, 2, T, HC), BF), dur=((NF, T, HC), BF),
-        at=((NF, 4 * Q, T), BF), atr=((NF, 2 * Q, T), BF),
+        a=((NF, T, D), BF), duf=((2, T, D), BF), u=((2, T, D), F32), g=((2, T, D), F32), du=((NF, 2, T, HC), BF), dur=((NF, T, HC), BF),
+        at=((NW, 4 * Q, TW), BF), atr=((NW, 4 * Q, TW), BF),
         oacc=((H, D), F32), dacc=((T, D), F32), dmid=((T, D), F32), gvec=((8, D), F32),
         dmb=((2, T, HC), BF), dmr=((T, HC), BF), dctx=((T, D), BF), draw=((2, 2 * J, T), BF),
         pd=((D // 128, 2, J, 128), BF), pdr=((D // 128, 2, J, 128), BF),
@@ -700,19 +784,21 @@
     if fused:
         scratch.update(
             parts,
-            wb1=((NF, Q, D), BF), wb2=((2, Q, D), BF), wb3=((Q, D), BF),
+            wb1=((2, 2 * Q, HC), BF), wb2=((2 * Q, HC), BF), finb=((2 * Q, HC), F32), finbr=((Q, HC), F32),
+            h2f=((T, D), BF), dyf=((T, D), BF), af=((2, T, D), BF),
             wi1=((NF, 4 * U, HC), BF), wi2=((NF, 2 * U, HC), BF), wi3=((NF, U, HC), BF),
             go1=((4 * U, HC), BF), go2=((2 * U, HC), BF), go3=((U, HC), BF),
             gq1=((4 * U, HC), BF), gq2=((2 * U, HC), BF), gq3=((U, HC), BF),
             gk1=((4 * U, HC), BF), gk2=((2 * U, HC), BF), gk3=((U, HC), BF),
-            gva1=((4 * U, GN // 2), BF), gva2=((2 * U, GN // 2), BF), gva3=((U, GN // 2), BF),
-            gvb1=((4 * U, GN // 2), BF), gvb2=((2 * U, GN // 2), BF), gvb3=((U, GN // 2), BF),
+            gva1=((4 * U, VW), BF), gva2=((2 * U, VW), BF), gva3=((U, VW), BF),
+            gvb1=((4 * U, HC - VW), BF), gvb2=((2 * U, HC - VW), BF), gvb3=((U, HC - VW), BF),
+            gg1=((4 * U, GN), BF), gg2=((2 * U, GN), BF), gg3=((U, GN), BF),
             ge1=((4 * EB, H), BF), ge2=((2 * EB, H), BF), ge3=((EB, H), BF),
-            fin=((U, NF * HC + 3 * HC + GN), F32), finr=((U // 2, NF * HC + 3 * HC + GN), F32),
+            fin=((U, NF * HC + 4 * HC + GN), F32), finr=((U // 2, NF * HC + 4 * HC + GN), F32),
         )
     counts = dict(
         x_seg=1, x_e=1, x_x=1, x_dy=1, c_pk=1, c_pv=1, c_h1t=1, c_h2t=1, c_dy=1, c_ctt=1, c_at=NF, c_du=NF, c_dm=1,
-        c_ds=D // 128, c_g=3, y_wb=NF, wi=3 * NF, lo_wb=2, hi_wb=1, go=3, gq=3, gk=3, gva=3, gvb=3, ge=3, c_fin=2,
+        c_ds=D // 256, c_g=3, y_wb=NF, wi=3 * NF, hi_wb=1, l_dy=1, x_dyf=1, l_h2=2, x_h2=2, c_finb=1, go=3, gq=3, gk=3, gva=3, gvb=3, gg=3, ge=3, c_fin=2,
     )
     sl, count = SimpleNamespace(), 0
     for name, n in counts.items():
@@ -733,7 +819,7 @@
         out_specs=[pl.BlockSpec(memory_space=pl.ANY if n[0] == "o" else pltpu.VMEM) for n in outs],
         scratch_shapes=[pltpu.VMEM(sh, dt) for sh, dt in scratch.values()]
         + [pltpu.SemaphoreType.DMA((10,))]
-        + [pltpu.SemaphoreType.DMA((14,)), pltpu.SemaphoreType.DMA((count,)), pltpu.SemaphoreType.DMA((count,))],
+        + [pltpu.SemaphoreType.DMA((13,)), pltpu.SemaphoreType.DMA((count,)), pltpu.SemaphoreType.DMA((count,))],
         compiler_params=pltpu.CompilerParams(
             collective_id=0, has_side_effects=True, vmem_limit_bytes=60 * 1024 * 1024
         ),
@@ -791,11 +877,11 @@
     wi = jnp.stack([whole(o.wi[f], True) for f in range(NF)], axis=1).reshape(D, FF)
     wo = whole(o.go, True)
     gv = jnp.concatenate([o.gva, o.gvb], axis=1)
-    wqkv = [whole(o.gq, True), whole(o.gk, True), whole(gv[:, :HC], True)]
-    gains = rows_back(gv[:, HC:], True)
+    wqkv = [whole(o.gq, True), whole(o.gk, True), whole(gv, True)]
+    gains = rows_back(o.gg, True)
     gfull = lax.dynamic_update_slice(jnp.zeros((8, 2, U, 128), F32), gains[:, None], (0, x, 0, 0)).reshape(D, 128)
-    wb = o.wb.astype(F32).reshape(NF * 2, 1, Q, D)
-    wb = lax.dynamic_update_slice(jnp.zeros((NF * 2, 4, Q, D), F32), wb, (0, s, 0, 0)).reshape(FF, D)
+    wb = o.wb.astype(F32).reshape(NF * 2, 1, 2 * Q, 1, HC)
+    wb = lax.dynamic_update_slice(jnp.zeros((NF * 2, 2, 2 * Q, 2, HC), F32), wb, (0, x, 0, c, 0)).reshape(FF, D)
     ge = o.ge.astype(F32).reshape(2, 2, 2, EB, H).transpose(2, 0, 1, 3, 4).reshape(J, H).T
     return (
         layer, x_grad, scatter(gfull[:, 0]), scatter(wqkv[0]), scatter(wqkv[1]), scatter(wqkv[2]), scatter(wo),

time: 75.9 us -> 72.3 us (0.953)
  Pallas kernels: 74.8 us -> 71.2 us
    pallas_call x1, Pallas kernels: 71.5 us -> 67.9 us  [run_layer(): pl.pallas_call(body, out_shape=[jax.ShapeDtypeStruct(sh, dt) for sh, dt i...]
where the time goes in v4:
time: 72.3 us; the launch traced here: 72 us
  Pallas kernels  71.2 us (98%)
  between operations  0.82 us (1%)
    pallas_call x1, Pallas kernels, run_layer(): pl.pallas_call(body, out_shape=[jax.ShapeDtypeStruct(sh, dt) for sh, dt i...  67.9 us
    pallas_call x1, Pallas kernels, run_layer(): pl.pallas_call(tail, out_shape=[jax.ShapeDtypeStruct(sh, dt) for sh, dt i...  3.27 us

profile of v4, /device:TPU:0, one launch (start us, length us, event | category | flops | bytes accessed | tf_op | source)
XLA Modules:
  0.0 72.0 jit_solution(14835899479529151125)
XLA Ops:
  0.6 67.9 %shard_map.230 = (bf16[128,768]{1,0:T(8,128)(2,1)}, f32[128,768]{1,0:T(8,128)}, f32[24,128]{1,0:T(8,128)}, f32[24,768]{1,0:T(8,128)}, f32[24,768]{1,0:T(8,128)},...) custom-call(bf16[128,768]{1,0:T(8,128)(2,1)} %bitcast.3, ...), custom_call_target="tpu_custom_call" | custom-call | flops 12000000000 | bytes 24000000 | tf_op jit(solution)/shard_map/pallas_call | solution.py:815
  68.6 3.3 %shard_map.231 = (bf16[1,128,768]{2,1,0:T(8,128)(2,1)}, f32[1,128,768]{2,1,0:T(8,128)}, f32[24,768]{1,0:T(8,128)}, f32[24,768]{1,0:T(8,128)}, f32[24,768]{1,0:T(...) custom-call(bf16[128,768]{1,0:T(8,128)(2,1)} %get-tuple-element.32.r, ...), custom_call_target="tpu_custom_call" | custom-call | tf_op jit(solution)/shard_map/pallas_call | solution.py:846

commit v5 on v4

--- a/solution.py
+++ b/solution.py
@@ -151,6 +151,16 @@
     r.q[own, :] = nn(r.h1[own, :], r.wq[...]).astype(BF)
     l_e.wait()
     l_sa.wait()
+    l_seg.wait()
+
+    def masks(part, at):
+        row = r.segs[part].astype(F32)
+        col = nt(eye[0:H, 0:H], jnp.broadcast_to(row, (J, H)).astype(BF))
+        r.sel_t[:, at] = jnp.where(slot_col[:, 0:H] == row, 1.0, 0.0)
+        r.me[at, :] = jnp.where(col == slot_row, r.eb[at, :].astype(F32), 0.0).astype(BF)
+        r.met[:, at] = nt(eye, r.me[at, :]).astype(BF)
+
+    masks(0, own)
     x_x.wait()
     x_dy.start()
     norm_into(r.xb, ga, r.xh1, r.rs1, r.h1, H, H)
@@ -158,12 +168,7 @@
 
     x_seg.wait()
     x_e.wait()
-    l_seg.wait()
-    seg_row = jnp.concatenate([r.segs[0], r.segs[1]], axis=1).astype(F32)
-    seg_col = nt(eye, jnp.broadcast_to(seg_row, (J, T)).astype(BF))
-    r.sel_t[...] = jnp.where(slot_col == seg_row, 1.0, 0.0)
-    r.me[...] = jnp.where(seg_col == slot_row, r.eb[...].astype(F32), 0.0).astype(BF)
-    r.met[...] = nt(eye, r.me[...]).astype(BF)
+    masks(1, far)
 
     c_pk = rc(sl.c_pk, r.pk.at[0], r.pkr.at[0], to_core)
     c_pv = rc(sl.c_pv, r.pk.at[1], r.pkr.at[1], to_core)
@@ -268,14 +273,14 @@
     EB = J // 8
     if fused:
         chain_w = [
-            (LYH if k % 2 else YLH, r.wi.at[k], (r.wi1.at[k], r.wi2.at[k], r.wi3.at[k]), sl.wi + 3 * k, U)
+            (LYH if k in (1, 3) else YLH, r.wi.at[k], (r.wi1.at[k], r.wi2.at[k], r.wi3.at[k]), sl.wi + 3 * k, U)
             for k in range(NF)
         ]
         chain_o = (LYH, r.go, (r.go1, r.go2, r.go3), sl.go, U)
         chain_q = (LYH, r.gq, (r.gq1, r.gq2, r.gq3), sl.gq, U)
         chain_k = (YLH, r.gk, (r.gk1, r.gk2, r.gk3), sl.gk, U)
         chain_va = (YLH, r.gva, (r.gva1, r.gva2, r.gva3), sl.gva, U)
-        chain_vb = (YLH, r.gvb, (r.gvb1, r.gvb2, r.gvb3), sl.gvb, U)
+        chain_vb = (LYH, r.gvb, (r.gvb1, r.gvb2, r.gvb3), sl.gvb, U)
         chain_g = (YLH, r.gg, (r.gg1, r.gg2, r.gg3), sl.gg, U)
         chain_e = (LYH, r.ge, (r.ge1, r.ge2, r.ge3), sl.ge, EB)
 
@@ -338,9 +343,7 @@
         MID_PUMPS = [[(w0, 0)], [(w1, 0)]]
         ATT_PUMPS = [[(w2, 0)], [(w0, 1), (w3, 0)], [], [], [(w1, 1)], []]
         KV_PUMPS = [[(chain_o, 0)], [], [(w2, 1), b0]]
-        END_PUMPS = [(w3, 1), b1, (chain_q, 0), (chain_e, 0), (chain_o, 1), (chain_k, 0), (chain_va, 0), (chain_vb, 0),
-                     (chain_g, 0), (chain_k, 1), (chain_va, 1), (chain_q, 1), (chain_vb, 1), (chain_e, 1),
-                     (chain_g, 1)]
+        END_PUMPS = [(w3, 1), b1, (chain_q, 0), (chain_vb, 0), (chain_e, 0), (chain_o, 1), (chain_k, 0), (chain_va, 0), (chain_g, 0), (chain_k, 1), (chain_q, 1), (chain_va, 1), (chain_vb, 1), (chain_e, 1), (chain_g, 1)]
 
     def swapped(buf, val, order, unit):
         if order == YLH:
@@ -543,6 +546,7 @@
         return rc(sl.c_g + i, r.dqkv.at[i, 1 - c], r.dqr.at[i], to_core)
 
     c_g(0).start()
+    r.dacc[...] = nt(r.dqkv[0, 0], r.wq[:, 0:HC]) + nt(r.dqkv[0, 1], r.wq[:, HC : 2 * HC])
     for i in range(D // 128):
         cols = slice(i * 128, (i + 1) * 128)
         if i % 2 == 0:
@@ -574,26 +578,22 @@
         b2, b1, b0 = b // 4, (b // 2) % 2, b % 2
         j = 4 * b0 + 2 * b2 + b1
         r.ge[b * EB : (b + 1) * EB, :] = de[j * EB : (j + 1) * EB, :]
-    acc = None
-    for i, w in enumerate((r.wq, r.wk, r.wv)):
-        if i == 1:
-            r.dacc[...] = acc
-            c_g(1).wait()
-            c_g(2).wait()
-            r.gk[...] = wgrad(1)
-            gv = wgrad(2)
-            r.gva[...] = gv[:, 0:VW]
-            r.gvb[...] = gv[:, VW:HC]
-            if fused:
-                st_copy(chain_k, 0).start()
-                st_copy(chain_va, 0).start()
-                st_copy(chain_vb, 0).start()
-                st_copy(chain_e, 0).start()
-                pump(KV_PUMPS[1])
-            acc = r.dacc[...]
+    c_g(1).wait()
+    c_g(2).wait()
+    swapped(r.gk, wgrad(1), YLH, U)
+    gv = wgrad(2)
+    swapped(r.gva, gv[:, 0:VW], YLH, U)
+    swapped(r.gvb, gv[:, VW:HC], LYH if fused else YLH, U)
+    if fused:
+        st_copy(chain_k, 0).start()
+        st_copy(chain_va, 0).start()
+        st_copy(chain_vb, 0).start()
+        st_copy(chain_e, 0).start()
+        pump(KV_PUMPS[1])
+    acc = r.dacc[...]
+    for i, w in ((1, r.wk), (2, r.wv)):
         for hf in range(2):
-            part = nt(r.dqkv[i, hf], w[:, hf * HC : (hf + 1) * HC])
-            acc = part if acc is None else acc + part
+            acc = acc + nt(r.dqkv[i, hf], w[:, hf * HC : (hf + 1) * HC])
     r.dacc[...] = acc
 
     gsum = None

time: 72.3 us -> 70.8 us (0.979)
  Pallas kernels: 71.2 us -> 69.1 us
    pallas_call x1, Pallas kernels: 67.9 us -> 65.9 us  [run_layer(): pl.pallas_call(body, out_shape=[jax.ShapeDtypeStruct(sh, dt) for sh, dt i...]
where the time goes in v5:
time: 70.8 us; the launch traced here: 69.9 us
  Pallas kernels  69.1 us (98%)
  between operations  0.82 us (1%)
    pallas_call x1, Pallas kernels, run_layer(): pl.pallas_call(body, out_shape=[jax.ShapeDtypeStruct(sh, dt) for sh, dt i...  65.9 us
    pallas_call x1, Pallas kernels, run_layer(): pl.pallas_call(tail, out_shape=[jax.ShapeDtypeStruct(sh, dt) for sh, dt i...  3.27 us

profile of v5, /device:TPU:0, one launch (start us, length us, event | category | flops | bytes accessed | tf_op | source)
XLA Modules:
  0.0 69.9 jit_solution(2927967421080971962)
XLA Ops:
  0.6 65.9 %shard_map.230 = (bf16[128,768]{1,0:T(8,128)(2,1)}, f32[128,768]{1,0:T(8,128)}, f32[24,128]{1,0:T(8,128)}, f32[24,768]{1,0:T(8,128)}, f32[24,768]{1,0:T(8,128)},...) custom-call(bf16[128,768]{1,0:T(8,128)(2,1)} %bitcast.3, ...), custom_call_target="tpu_custom_call" | custom-call | flops 12000000000 | bytes 24000000 | tf_op jit(solution)/shard_map/pallas_call | solution.py:815
  66.5 3.3 %shard_map.231 = (bf16[1,128,768]{2,1,0:T(8,128)(2,1)}, f32[1,128,768]{2,1,0:T(8,128)}, f32[24,768]{1,0:T(8,128)}, f32[24,768]{1,0:T(8,128)}, f32[24,768]{1,0:T(...) custom-call(bf16[128,768]{1,0:T(8,128)(2,1)} %get-tuple-element.32.r, ...), custom_call_target="tpu_custom_call" | custom-call | tf_op jit(solution)/shard_map/pallas_call | solution.py:846

commit v6 on v5

--- a/solution.py
+++ b/solution.py
@@ -342,8 +342,8 @@
         FFN_PUMPS = [[], [], [h0], [h1]]
         MID_PUMPS = [[(w0, 0)], [(w1, 0)]]
         ATT_PUMPS = [[(w2, 0)], [(w0, 1), (w3, 0)], [], [], [(w1, 1)], []]
-        KV_PUMPS = [[(chain_o, 0)], [], [(w2, 1), b0]]
-        END_PUMPS = [(w3, 1), b1, (chain_q, 0), (chain_vb, 0), (chain_e, 0), (chain_o, 1), (chain_k, 0), (chain_va, 0), (chain_g, 0), (chain_k, 1), (chain_q, 1), (chain_va, 1), (chain_vb, 1), (chain_e, 1), (chain_g, 1)]
+        KV_PUMPS = [[(chain_o, 0)], [b0, (w2, 1)], [b1, (chain_q, 0)]]
+        END_PUMPS = [(w3, 1), (chain_vb, 0), (chain_e, 0), (chain_o, 1), (chain_k, 0), (chain_q, 1), (chain_va, 0), (chain_k, 1), (chain_g, 0), (chain_va, 1), (chain_vb, 1), (chain_e, 1), (chain_g, 1)]
 
     def swapped(buf, val, order, unit):
         if order == YLH:

time: 70.8 us -> 69.3 us (0.979)
  Pallas kernels: 69.1 us -> 68.3 us
    pallas_call x1, Pallas kernels: 65.9 us -> 65 us  [run_layer(): pl.pallas_call(body, out_shape=[jax.ShapeDtypeStruct(sh, dt) for sh, dt i...]
where the time goes in v6:
time: 69.3 us; the launch traced here: 69.1 us
  Pallas kernels  68.3 us (99%)
  between operations  0.82 us (1%)
    pallas_call x1, Pallas kernels, run_layer(): pl.pallas_call(body, out_shape=[jax.ShapeDtypeStruct(sh, dt) for sh, dt i...  65 us
    pallas_call x1, Pallas kernels, run_layer(): pl.pallas_call(tail, out_shape=[jax.ShapeDtypeStruct(sh, dt) for sh, dt i...  3.27 us

profile of v6, /device:TPU:0, one launch (start us, length us, event | category | flops | bytes accessed | tf_op | source)
XLA Modules:
  0.0 69.1 jit_solution(16330309025180040258)
XLA Ops:
  0.6 65.0 %shard_map.230 = (bf16[128,768]{1,0:T(8,128)(2,1)}, f32[128,768]{1,0:T(8,128)}, f32[24,128]{1,0:T(8,128)}, f32[24,768]{1,0:T(8,128)}, f32[24,768]{1,0:T(8,128)},...) custom-call(bf16[128,768]{1,0:T(8,128)(2,1)} %bitcast.3, ...), custom_call_target="tpu_custom_call" | custom-call | flops 12000000000 | bytes 24000000 | tf_op jit(solution)/shard_map/pallas_call | solution.py:815
  65.7 3.3 %shard_map.231 = (bf16[1,128,768]{2,1,0:T(8,128)(2,1)}, f32[1,128,768]{2,1,0:T(8,128)}, f32[24,768]{1,0:T(8,128)}, f32[24,768]{1,0:T(8,128)}, f32[24,768]{1,0:T(...) custom-call(bf16[128,768]{1,0:T(8,128)(2,1)} %get-tuple-element.32.r, ...), custom_call_target="tpu_custom_call" | custom-call | tf_op jit(solution)/shard_map/pallas_call | solution.py:846

commit v7 on v6

--- a/solution.py
+++ b/solution.py
@@ -629,6 +629,7 @@
     first = (w0, w1, w2, w3, chain_o, chain_q, chain_k)
     homes = [(r.s_in, k * FC) for k in range(NF)] + [(r.s_out, 0), (r.s_q, 0), (r.s_k, 0), (r.s_v, 0)]
     n1 = len(first) * HC
+    n0 = (NF + 1) * HC
 
     def send_out(src, dst):
         cp = pltpu.make_async_copy(src, dst, r.osem.at[len(outs)])
@@ -636,7 +637,7 @@
         outs.append(cp)
 
     def c_fin(i):
-        cols = pl.ds(0, n1) if i == 0 else pl.ds(n1, HC + GN)
+        cols = (pl.ds(n0, n1 + VW - n0), pl.ds(n1 + VW, HC - VW + GN), pl.ds(0, n0))[i]
         rows = pl.ds(pl.multiple_of((1 - c) * half, 8), half)
         return rc(sl.c_fin + i, fin.at[rows, cols], r.finr.at[:, cols], to_core)
 
@@ -655,8 +656,9 @@
     r.finb[...] = r.wb[hi, rows16(y * 2 * Q, 2 * Q), :].astype(F32) + r.wb2[...].astype(F32)
     c_finb = rc(sl.c_finb, r.finb.at[pl.ds(pl.multiple_of((1 - c) * Q, 8), Q)], r.finbr, to_core)
     c_finb.start()
-    for i in (4, 6):
-        take(i)
+    take(4)
+    c_fin(2).start()
+    take(6)
     fin[:, n1 : n1 + VW] = st_last(chain_va)
     take(5)
     c_fin(0).start()
@@ -669,11 +671,16 @@
     r.s_back[:, pl.ds(pl.multiple_of(c * HC, 128), HC)] = r.finb[pl.ds(pl.multiple_of(c * Q, 8), Q), :]
     r.s_back[:, pl.ds(pl.multiple_of((1 - c) * HC, 128), HC)] = r.finbr[...]
     send_out(r.s_back, r.o_back)
+    c_fin(2).wait()
+    for i in range(NF + 1):
+        put(i)
+    send_out(r.s_in, r.o_in)
+    send_out(r.s_out, r.o_out)
     c_fin(0).wait()
-    for i in range(len(first)):
+    for i in (NF + 1, NF + 2):
         put(i)
-    for src, dst in ((r.s_in, r.o_in), (r.s_out, r.o_out), (r.s_q, r.o_q), (r.s_k, r.o_k)):
-        send_out(src, dst)
+    send_out(r.s_q, r.o_q)
+    send_out(r.s_k, r.o_k)
     c_fin(1).wait()
     put(len(first))
     at = n1 + HC
@@ -689,17 +696,12 @@
 
 
 def hand_over(r, names):
-    copies = []
-    for i, (src, dst) in enumerate(names):
-        cp = pltpu.make_async_copy(src, dst, r.sem.at[i])
-        cp.start()
-        copies.append(cp)
+    for src, dst in names:
+        dst[...] = src[...]
     g = jnp.concatenate([r.s_g[...], jnp.zeros((128 - r.s_g.shape[0], 128), F32)], axis=0).T
     n = r.s_g.shape[0]
     r.d_ga[...] = g[0, 0:n]
     r.d_gf[...] = g[1, 0:n]
-    for cp in copies:
-        cp.wait()
 
 
 def run_layer(mesh_shape, tokens, seg_ids, slot_doc, proj_e, g_attn, w_query, w_key, w_value, w_out, g_ffn, w_in,
@@ -798,7 +800,7 @@
         )
     counts = dict(
         x_seg=1, x_e=1, x_x=1, x_dy=1, c_pk=1, c_pv=1, c_h1t=1, c_h2t=1, c_dy=1, c_ctt=1, c_at=NF, c_du=NF, c_dm=1,
-        c_ds=D // 256, c_g=3, y_wb=NF, wi=3 * NF, hi_wb=1, l_dy=1, x_dyf=1, l_h2=2, x_h2=2, c_finb=1, go=3, gq=3, gk=3, gva=3, gvb=3, gg=3, ge=3, c_fin=2,
+        c_ds=D // 256, c_g=3, y_wb=NF, wi=3 * NF, hi_wb=1, l_dy=1, x_dyf=1, l_h2=2, x_h2=2, c_finb=1, go=3, gq=3, gk=3, gva=3, gvb=3, gg=3, ge=3, c_fin=3,
     )
     sl, count = SimpleNamespace(), 0
     for name, n in counts.items():
@@ -846,7 +848,7 @@
         res = pl.pallas_call(
             tail,
             out_shape=[jax.ShapeDtypeStruct(sh, dt) for sh, dt in dst.values()],
-            in_specs=[pl.BlockSpec(memory_space=pl.ANY)] * n_copy + [pl.BlockSpec(memory_space=pltpu.VMEM)],
+            in_specs=[pl.BlockSpec(memory_space=pltpu.VMEM)] * len(src),
             out_specs=[pl.BlockSpec(memory_space=pltpu.VMEM)] * len(dst),
             scratch_shapes=[pltpu.SemaphoreType.DMA((n_copy,))],
         )(*src.values())

time: 69.3 us -> 68.5 us (0.988)
  Pallas kernels: 68.3 us -> 67.6 us
    pallas_call x1, Pallas kernels: 3.27 us -> 2.57 us  [run_layer(): pl.pallas_call(tail, out_shape=[jax.ShapeDtypeStruct(sh, dt) for sh, dt i...]
where the time goes in v7:
time: 68.5 us; the launch traced here: 68.4 us
  Pallas kernels  67.6 us (99%)
  between operations  0.82 us (1%)
    pallas_call x1, Pallas kernels, run_layer(): pl.pallas_call(body, out_shape=[jax.ShapeDtypeStruct(sh, dt) for sh, dt i...  65 us
    pallas_call x1, Pallas kernels, run_layer(): pl.pallas_call(tail, out_shape=[jax.ShapeDtypeStruct(sh, dt) for sh, dt i...  2.57 us

profile of v7, /device:TPU:0, one launch (start us, length us, event | category | flops | bytes accessed | tf_op | source)
XLA Modules:
  0.0 68.4 jit_solution(13322184277243011011)
XLA Ops:
  0.6 65.0 %shard_map.230 = (bf16[128,768]{1,0:T(8,128)(2,1)}, f32[128,768]{1,0:T(8,128)}, f32[24,128]{1,0:T(8,128)}, f32[24,768]{1,0:T(8,128)}, f32[24,768]{1,0:T(8,128)},...) custom-call(bf16[128,768]{1,0:T(8,128)(2,1)} %bitcast.3, ...), custom_call_target="tpu_custom_call" | custom-call | flops 12000000000 | bytes 24000000 | tf_op jit(solution)/shard_map/pallas_call | solution.py:817
  65.6 2.6 %shard_map.231 = (bf16[1,128,768]{2,1,0:T(8,128)(2,1)}, f32[1,128,768]{2,1,0:T(8,128)}, f32[24,768]{1,0:T(8,128)}, f32[24,768]{1,0:T(8,128)}, f32[24,768]{1,0:T(...) custom-call(bf16[128,768]{1,0:T(8,128)(2,1)} %get-tuple-element.32.r, ...), custom_call_target="tpu_custom_call" | custom-call | tf_op jit(solution)/shard_map/pallas_call | solution.py:848
